TPU v7x, 128 devices: a whole 4x4x4 slice. The times are simulated.
128 devices in a mesh: pipe: 8 (over x_lo, y), tensor: 8 (over z, core), dp: 2 (over x_hi).
Axes of the slice: x: 4 (x_hi: 2, x_lo: 2; x = x_hi * 2 + x_lo), y: 4, z: 4, core: 2. Of those that a mesh axis runs over, the one named last changes fastest.
Arguments:
- inputs: bfloat16 [2, 256, 2560], P(None, 'dp'), may hold values from -60 to 60
- cotangent: bfloat16 [2, 256, 2560], P(None, 'dp'), may hold values from -6 to 6
- lengths: int32 [2, 2, 4], P(None, 'dp'), may hold values from 1 to 64, 128 in all within a row
- down_qkv: bfloat16 [8, 2560, 3, 3072], P('pipe', None, None, 'tensor'), may hold values from -6 to 6
- down_out: bfloat16 [8, 2560, 3072], P('pipe', None, 'tensor'), may hold values from -0.109375 to 0.109375
- down_gain: bfloat16 [8, 2560], P('pipe'), may hold values from 0.099609375 to 1.8984375
- up_qkv: bfloat16 [8, 2560, 3, 3072], P('pipe', None, None, 'tensor'), may hold values from -6 to 6
- up_out: bfloat16 [8, 2560, 3072], P('pipe', None, 'tensor'), may hold values from -0.109375 to 0.109375
- up_gain: bfloat16 [8, 2560], P('pipe'), may hold values from 0.099609375 to 1.8984375
Outputs:
- grad_qkv: float32 [8, 2560, 3, 3072], P('pipe', 'dp', None, 'tensor')
- grad_out: float32 [8, 2560, 3072], P('pipe', 'dp', 'tensor')
Inputs may be any that keep to these rules, and one draw needn't show every extreme that they name: Each row holds 4 document lengths of one micro-batch that sum to 128; the longest is exactly 64.
All inputs are finite; a program needn't handle non-finite values.
Results may differ from a plain program's by a relative error of at most 0.039.
Values may be sent and summed in bfloat16 or wider, within the bound.
No kernel may reach another device: no remote copies, remote signals or barrier semaphores. Data moves between devices by JAX's collectives and lax.ppermute only.
A program may use at most 256 MiB of HBM per device.

v0:
```python
import jax
import jax.numpy as jnp
from jax import lax
from jax.sharding import PartitionSpec as P

HS = 128


norm_epsilon = 1e-05


def for_sending(x):
    return jax.tree.map(lambda a: a.astype(jnp.bfloat16) if a.dtype == jnp.float32 else a, x)


def passed_along(block, axis, distance):
    devices = range(lax.axis_size(axis))
    route = [(i - distance, i) for i in devices if i - distance in devices]
    return lax.ppermute(block, axis, route)


def from_partner(value, axis, distance):
    mask = 2**distance
    pairs = [(source, source ^ mask) for source in range(lax.axis_size(axis))]
    return lax.ppermute(value, axis, pairs)


def doc_mask(doc_lengths, row_count):
    doc_ends = jnp.cumsum(doc_lengths)
    places = jnp.arange(row_count, dtype=jnp.int32)
    segment = jnp.sum((places[:, None] >= doc_ends[None, :]).astype(jnp.int32), axis=1)
    return (segment[:, None] == segment[None, :]) & (places[None, :] <= places[:, None])


def normalize(section_input, gain_vector):
    floated = section_input.astype(jnp.float32)
    centred = floated - jnp.mean(floated, axis=-1, keepdims=True)
    inv_scale = lax.rsqrt(jnp.mean(centred * centred, axis=-1, keepdims=True) + norm_epsilon)
    normed = (centred * inv_scale * gain_vector).astype(jnp.bfloat16)
    return (normed, centred, inv_scale)


def attend(normed, group_cols, allowed):
    row_count = normed.shape[0]
    group_width = group_cols.shape[1] // 3
    heads_here = group_width // HS
    factor = HS ** (-0.5)
    projected = jnp.dot(normed, group_cols, preferred_element_type=jnp.float32).astype(jnp.bfloat16)
    projected = projected.reshape(row_count, 3, heads_here, HS)
    queries = projected[:, 0]
    key_rows = projected[:, 1]
    values = projected[:, 2]
    scores = (
        jnp.einsum("thd,shd->hts", queries, key_rows, preferred_element_type=jnp.float32) * factor
    )
    scores = jnp.where(allowed[None], scores, -1e30)
    highest = jnp.max(scores, axis=-1, keepdims=True)
    raised = jnp.exp(scores - highest)
    probability = raised / jnp.sum(raised, axis=-1, keepdims=True)
    weights = probability.astype(jnp.bfloat16)
    context = jnp.einsum("hts,shd->thd", weights, values, preferred_element_type=jnp.float32)
    context = context.astype(jnp.bfloat16).reshape(row_count, group_width)
    return (queries, key_rows, values, probability, weights, context)


def attend_back(out_grad, group_cols, group_out, cached, need_input):
    queries, key_rows, values, probability, weights, context = cached
    row_count = out_grad.shape[0]
    group_width = group_out.shape[1]
    heads_here = group_width // HS
    factor = HS ** (-0.5)
    ctx_grad = jnp.dot(out_grad, group_out, preferred_element_type=jnp.float32).astype(jnp.bfloat16)
    ctx_grad = ctx_grad.reshape(row_count, heads_here, HS)
    prob_grad = jnp.einsum("thd,shd->hts", ctx_grad, values, preferred_element_type=jnp.float32)
    inner_sum = jnp.sum(probability * prob_grad, axis=-1, keepdims=True)
    score_grad = (probability * (prob_grad - inner_sum) * factor).astype(jnp.bfloat16)
    query_grad = jnp.einsum(
        "hts,shd->thd", score_grad, key_rows, preferred_element_type=jnp.float32
    )
    key_grad = jnp.einsum("hts,thd->shd", score_grad, queries, preferred_element_type=jnp.float32)
    value_grad = jnp.einsum("hts,thd->shd", weights, ctx_grad, preferred_element_type=jnp.float32)
    qkv_grad = jnp.stack([query_grad, key_grad, value_grad], axis=1).reshape(
        row_count, 3 * group_width
    )
    qkv_grad = qkv_grad.astype(jnp.bfloat16)
    if need_input:
        normed_grad = lax.dot_general(
            qkv_grad, group_cols, (((1,), (1,)), ((), ())), preferred_element_type=jnp.float32
        )
    else:
        normed_grad = jnp.zeros((row_count, group_cols.shape[0]), jnp.float32)
    return (normed_grad, qkv_grad, context)


def norm_back(normed_grad, centred, inv_scale, gain_vector):
    scaled = normed_grad * gain_vector
    unit_rows = centred * inv_scale
    first_mean = jnp.mean(scaled, axis=-1, keepdims=True)
    second_mean = jnp.mean(scaled * unit_rows, axis=-1, keepdims=True)
    return inv_scale * (scaled - first_mean - unit_rows * second_mean)


def make_front(group_cols, group_out, gain_vector, allowed):

    def run_section(section_input):
        normed, _, _ = normalize(section_input, gain_vector)
        context = attend(normed, group_cols, allowed)[5]
        return lax.dot_general(
            context, group_out, (((1,), (1,)), ((), ())), preferred_element_type=jnp.float32
        )

    return run_section


def make_spare_front(row_count, model_width):

    def spare_section(section_input):
        return jnp.zeros((row_count, model_width), jnp.float32)

    return spare_section


def make_back(group_cols, group_out, gain_vector, allowed, need_input):

    def run_section(section_input, out_grad):
        normed, _, _ = normalize(section_input, gain_vector)
        cached = attend(normed, group_cols, allowed)
        normed_grad, qkv_grad, context = attend_back(
            out_grad, group_cols, group_out, cached, need_input
        )
        return (normed_grad, normed, qkv_grad, context)

    return run_section


def make_spare_back(row_count, model_width, group_width):

    def spare_section(section_input, out_grad):
        return (
            jnp.zeros((row_count, model_width), jnp.float32),
            jnp.zeros((row_count, model_width), jnp.bfloat16),
            jnp.zeros((row_count, 3 * group_width), jnp.bfloat16),
            jnp.zeros((row_count, group_width), jnp.bfloat16),
        )

    return spare_section


def select_items(flag, fresh_items, kept_items):
    return tuple(
        (
            jnp.where(flag, fresh_part, kept_part)
            for fresh_part, kept_part in zip(fresh_items, kept_items)
        )
    )


def contract_rows(left_rows, right_rows):
    return lax.dot_general(
        left_rows, right_rows, (((0,), (0,)), ((), ())), preferred_element_type=jnp.float32
    )


def local(inputs, cotangent, lengths, down_qkv, down_out, down_gain, up_qkv, up_out, up_gain):
    sections = lax.axis_size("pipe")
    section_place = lax.axis_index("pipe")
    row_count = inputs.shape[1]
    model_width = down_out.shape[1]
    group_width = down_out.shape[2]
    down_cols = down_qkv[0].reshape(model_width, 3 * group_width)
    up_cols = up_qkv[0].reshape(model_width, 3 * group_width)
    down_scale = down_gain[0].astype(jnp.float32)
    up_scale = up_gain[0].astype(jnp.float32)
    down_allowed = doc_mask(lengths[0, 0], row_count)
    up_allowed = doc_mask(lengths[1, 0], row_count)
    front_branches = [
        make_spare_front(row_count, model_width),
        make_front(down_cols, down_out[0], down_scale, down_allowed),
        make_front(up_cols, up_out[0], up_scale, up_allowed),
    ]
    down_buffer = inputs[0]
    up_buffer = inputs[1]
    saved_down = jnp.zeros_like(inputs[0])
    saved_up = jnp.zeros_like(inputs[1])
    for step_index in range(sections):
        is_down = section_place == step_index
        is_up = section_place == sections - 1 - step_index
        chosen = jnp.where(is_down, down_buffer, up_buffer)
        section_input = chosen
        saved_down = jnp.where(is_down, section_input, saved_down)
        saved_up = jnp.where(is_up, section_input, saved_up)
        if step_index < sections - 1:
            section_role = jnp.where(is_down, 1, jnp.where(is_up, 2, 0)).astype(jnp.int32)
            partial_value = lax.switch(section_role, front_branches, section_input)
            summed_out = jax.tree.map(
                lambda part: part.astype(jnp.float32),
                lax.psum(for_sending(partial_value), "tensor"),
            )
            result = (section_input.astype(jnp.float32) + summed_out).astype(jnp.bfloat16)
            down_buffer = passed_along(result, "pipe", 1)
            up_buffer = passed_along(result, "pipe", -1)
    empty_items = (
        jnp.zeros((row_count, model_width), jnp.bfloat16),
        jnp.zeros((row_count, 3 * group_width), jnp.bfloat16),
        jnp.zeros((row_count, group_width), jnp.bfloat16),
        jnp.zeros((row_count, model_width), jnp.bfloat16),
    )
    down_keep = empty_items
    up_keep = empty_items
    grad_down = cotangent[0]
    grad_up = cotangent[1]
    for step_index in range(sections):
        is_down = section_place == sections - 1 - step_index
        is_up = section_place == step_index
        need_input = step_index < sections - 1
        chosen = jnp.where(is_down, grad_down, grad_up)
        section_input = jnp.where(is_down, saved_down, saved_up)
        section_role = jnp.where(is_down, 1, jnp.where(is_up, 2, 0)).astype(jnp.int32)
        back_branches = [
            make_spare_back(row_count, model_width, group_width),
            make_back(down_cols, down_out[0], down_scale, down_allowed, need_input),
            make_back(up_cols, up_out[0], up_scale, up_allowed, need_input),
        ]
        normed_grad, normed, qkv_grad, context = lax.switch(
            section_role, back_branches, section_input, chosen
        )
        fresh_items = (normed, qkv_grad, context, chosen)
        down_keep = select_items(is_down, fresh_items, down_keep)
        up_keep = select_items(is_up, fresh_items, up_keep)
        if need_input:
            gain_vector = jnp.where(is_down, down_scale, up_scale)
            summed_grad = jax.tree.map(
                lambda part: part.astype(jnp.float32), lax.psum(for_sending(normed_grad), "tensor")
            )
            _, centred, inv_scale = normalize(section_input, gain_vector)
            result = (
                chosen.astype(jnp.float32) + norm_back(summed_grad, centred, inv_scale, gain_vector)
            ).astype(jnp.bfloat16)
            grad_down = passed_along(result, "pipe", -1)
            grad_up = passed_along(result, "pipe", 1)
    replicas = lax.axis_size("dp")
    rows_here = model_width // replicas
    bit_count = sections.bit_length() - 1
    qkv_cols = 3 * group_width
    packed = jnp.concatenate(up_keep, axis=1)
    for bit_index in range(bit_count):
        packed = from_partner(for_sending(packed), "pipe", bit_index).astype(packed.dtype)
    cut_two = model_width + qkv_cols
    cut_three = cut_two + group_width
    normed_all = jnp.concatenate([down_keep[0], packed[:, :model_width]], axis=0)
    qkv_all = jnp.concatenate([down_keep[1], packed[:, model_width:cut_two]], axis=0)
    context_all = jnp.concatenate([down_keep[2], packed[:, cut_two:cut_three]], axis=0)
    grad_all = jnp.concatenate([down_keep[3], packed[:, cut_three:]], axis=0)
    normed_rows = lax.slice_in_dim(normed_all, 0, rows_here * lax.axis_size("dp"), axis=1)
    grad_rows = lax.slice_in_dim(grad_all, 0, rows_here * lax.axis_size("dp"), axis=1)
    summed_total = lax.psum_scatter(
        jnp.concatenate(
            [contract_rows(normed_rows, qkv_all), contract_rows(grad_rows, context_all)], axis=1
        ).astype(jnp.bfloat16),
        "dp",
        scatter_dimension=0,
        tiled=True,
    ).astype(jnp.float32)
    summed_total = summed_total / replicas
    grad_qkv = summed_total[:, :qkv_cols].reshape(1, rows_here, 3, group_width)
    grad_out = summed_total[:, qkv_cols:].reshape(1, rows_here, group_width)
    return (grad_qkv, grad_out)


def solution(mesh):
    placed = (
        P(None, "dp", None),
        P(None, "dp", None),
        P(None, "dp", None),
        P("pipe", None, None, "tensor"),
        P("pipe", None, "tensor"),
        P("pipe", None),
        P("pipe", None, None, "tensor"),
        P("pipe", None, "tensor"),
        P("pipe", None),
    )
    return jax.shard_map(
        local,
        mesh=mesh,
        in_specs=placed,
        out_specs=(P("pipe", "dp", None, "tensor"), P("pipe", "dp", "tensor")),
        check_vma=False,
    )
```

profile of v0, /device:TPU:1, one launch (start us, length us, event | category | flops | bytes accessed | tf_op | source)
XLA Modules:
  0.0 1929.7 jit_solution(2993897044223270806)
XLA Ops:
  39.5 64.9 %all-reduce.15.cloned.1.call-done = bf16[128,2560]{0,1:T(8,128)(2,1)} async-done(((bf16[128,2560]{0,1:T(8,128)(2,1)}), bf16[128,2560]{0,1:T(8,128)(2,1)}) %all-reduce.15.cloned.1.call-update) | async-done | bytes 655376 | tf_op jit(solution)/shard_map/psum | solution.py:197
  111.0 10.2 collective-permute-done
  136.8 79.4 %all-reduce.17.cloned.1.call-done = bf16[128,2560]{0,1:T(8,128)(2,1)} async-done(((bf16[128,2560]{0,1:T(8,128)(2,1)}), bf16[128,2560]{0,1:T(8,128)(2,1)}) %all-reduce.17.cloned.1.call-update) | async-done | bytes 655376 | tf_op jit(solution)/shard_map/psum | solution.py:197
  222.7 10.2 collective-permute-done.2
  241.3 80.4 %all-reduce.19.cloned.1.call-done = bf16[128,2560]{0,1:T(8,128)(2,1)} async-done(((bf16[128,2560]{0,1:T(8,128)(2,1)}), bf16[128,2560]{0,1:T(8,128)(2,1)}) %all-reduce.19.cloned.1.call-update) | async-done | bytes 655376 | tf_op jit(solution)/shard_map/psum | solution.py:197
  354.2 82.3 %all-reduce.21.cloned.1.call-done = bf16[128,2560]{0,1:T(8,128)(2,1)} async-done(((bf16[128,2560]{0,1:T(8,128)(2,1)}), bf16[128,2560]{0,1:T(8,128)(2,1)}) %all-reduce.21.cloned.1.call-update) | async-done | bytes 655376 | tf_op jit(solution)/shard_map/psum | solution.py:197
  443.1 10.2 collective-permute-done.6
  461.6 82.9 %all-reduce.23.cloned.1.call-done = bf16[128,2560]{0,1:T(8,128)(2,1)} async-done(((bf16[128,2560]{0,1:T(8,128)(2,1)}), bf16[128,2560]{0,1:T(8,128)(2,1)}) %all-reduce.23.cloned.1.call-update) | async-done | bytes 655376 | tf_op jit(solution)/shard_map/psum | solution.py:197
  551.1 10.2 collective-permute-done.8
  576.8 79.0 %all-reduce.25.cloned.1.call-done = bf16[128,2560]{0,1:T(8,128)(2,1)} async-done(((bf16[128,2560]{0,1:T(8,128)(2,1)}), bf16[128,2560]{0,1:T(8,128)(2,1)}) %all-reduce.25.cloned.1.call-update) | async-done | bytes 655376 | tf_op jit(solution)/shard_map/psum | solution.py:197
  687.9 73.2 %all-reduce.27.cloned.1.call-done = bf16[128,2560]{0,1:T(8,128)(2,1)} async-done(((bf16[128,2560]{0,1:T(8,128)(2,1)}), bf16[128,2560]{0,1:T(8,128)(2,1)}) %all-reduce.27.cloned.1.call-update) | async-done | bytes 655376 | tf_op jit(solution)/shard_map/psum | solution.py:197
  786.8 36.6 %conditional.22 = (bf16[128,2560]{1,0:T(8,128)(2,1)}, bf16[128,1152]{0,1:T(8,128)(2,1)}, bf16[128,384]{0,1:T(8,128)(2,1)}, bf16[128,2560]{0,1:T(8,128)(2,1)}) conditional(s32[]{:T(128)} %clamp.38, () %tuple.189, (bf16[128,2560]{0,1:T(8,128)(2,1)S(1)}, f32[2560]{0:T(1024)S(1)}, bf16[2560,1152]{0,1:T(8,128)(2,1)}, ...), branch_computations={%region_90.91_spmd, %region_91.0_spmd, %region_97.0_spmd} | conditional | flops 1842579712 | bytes 32452184 | solution.py:224
  826.1 61.7 %all-reduce.29.cloned.1.call-done = bf16[128,2560]{0,1:T(8,128)(2,1)} async-done(((bf16[128,2560]{0,1:T(8,128)(2,1)}), bf16[128,2560]{0,1:T(8,128)(2,1)}) %all-reduce.29.cloned.1.call-update) | async-done | bytes 655376 | tf_op jit(solution)/shard_map/psum | solution.py:233
  913.5 96.0 %all-reduce.31.cloned.1.call-done = bf16[128,2560]{0,1:T(8,128)(2,1)} async-done(((bf16[128,2560]{0,1:T(8,128)(2,1)}), bf16[128,2560]{0,1:T(8,128)(2,1)}) %all-reduce.31.cloned.1.call-update) | async-done | bytes 655376 | tf_op jit(solution)/shard_map/psum | solution.py:233
  1036.6 97.3 %all-reduce.33.cloned.1.call-done = bf16[128,2560]{0,1:T(8,128)(2,1)} async-done(((bf16[128,2560]{0,1:T(8,128)(2,1)}), bf16[128,2560]{0,1:T(8,128)(2,1)}) %all-reduce.33.cloned.1.call-update) | async-done | bytes 655376 | tf_op jit(solution)/shard_map/psum | solution.py:233
  1161.8 97.9 %all-reduce.35.cloned.1.call-done = bf16[128,2560]{0,1:T(8,128)(2,1)} async-done(((bf16[128,2560]{0,1:T(8,128)(2,1)}), bf16[128,2560]{0,1:T(8,128)(2,1)}) %all-reduce.35.cloned.1.call-update) | async-done | bytes 655376 | tf_op jit(solution)/shard_map/psum | solution.py:233
  1287.6 98.9 %all-reduce.37.cloned.1.call-done = bf16[128,2560]{0,1:T(8,128)(2,1)} async-done(((bf16[128,2560]{0,1:T(8,128)(2,1)}), bf16[128,2560]{0,1:T(8,128)(2,1)}) %all-reduce.37.cloned.1.call-update) | async-done | bytes 655376 | tf_op jit(solution)/shard_map/psum | solution.py:233
  1414.6 96.4 %all-reduce.39.cloned.1.call-done = bf16[128,2560]{0,1:T(8,128)(2,1)} async-done(((bf16[128,2560]{0,1:T(8,128)(2,1)}), bf16[128,2560]{0,1:T(8,128)(2,1)}) %all-reduce.39.cloned.1.call-update) | async-done | bytes 655376 | tf_op jit(solution)/shard_map/psum | solution.py:233
  1538.9 96.8 %all-reduce.41.cloned.1.call-done = bf16[128,2560]{0,1:T(8,128)(2,1)} async-done(((bf16[128,2560]{0,1:T(8,128)(2,1)}), bf16[128,2560]{0,1:T(8,128)(2,1)}) %all-reduce.41.cloned.1.call-update) | async-done | bytes 655376 | tf_op jit(solution)/shard_map/psum | solution.py:233
  1673.2 34.8 %collective-permute-done.28 = bf16[128,6656]{0,1:T(8,128)(2,1)S(1)} collective-permute-done((bf16[128,6656]{0,1:T(8,128)(2,1)S(1)}, bf16[128,6656]{0,1:T(8,128)(2,1)S(1)}, u32[]{:S(2)}, u32[]{:S(2)}) %collective-permute-start.28) | collective-permute-done | bytes 1703968 | tf_op jit(solution)/shard_map/ppermute | solution.py:25
  1707.9 32.6 %collective-permute-done.29 = bf16[128,6656]{0,1:T(8,128)(2,1)S(1)} collective-permute-done((bf16[128,6656]{0,1:T(8,128)(2,1)S(1)}, bf16[128,6656]{0,1:T(8,128)(2,1)S(1)}, u32[]{:S(2)}, u32[]{:S(2)}) %collective-permute-start.29) | collective-permute-done | bytes 1703968 | tf_op jit(solution)/shard_map/ppermute | solution.py:25
  1740.5 10.4 collective-permute-start.30
  1750.9 33.1 %collective-permute-done.30 = bf16[128,6656]{0,1:T(8,128)(2,1)S(1)} collective-permute-done((bf16[128,6656]{0,1:T(8,128)(2,1)S(1)}, bf16[128,6656]{0,1:T(8,128)(2,1)S(1)}, u32[]{:S(2)}, u32[]{:S(2)}) %collective-permute-start.30) | collective-permute-done | bytes 1703968 | tf_op jit(solution)/shard_map/ppermute | solution.py:25
  1797.4 110.4 %reduce-scatter.2.cloned.1.call-done = bf16[1280,1536]{0,1:T(8,128)(2,1)} async-done(((bf16[2560,1536]{0,1:T(8,128)(2,1)}), bf16[1280,1536]{0,1:T(8,128)(2,1)}) %reduce-scatter.2.cloned.1.call-update) | async-done | bytes 3932176 | tf_op jit(solution)/shard_map/reduce_scatter | solution.py:256
  (422 shorter events, 507.3 us)
Async XLA Ops:
  7.2 97.3 %all-reduce.15.cloned.1.call-start = ((), (), s32[]{:S(2)}) async-start(), calls=%async_computation.1 | async-start | bytes 1310720 | tf_op jit(solution)/shard_map/psum | solution.py:197
  39.5 176.7 %all-reduce.17.cloned.1.call-start = ((), (), s32[]{:S(2)}) async-start(), calls=%async_computation.2 | async-start | bytes 1310720 | tf_op jit(solution)/shard_map/psum | solution.py:197
  109.7 15.4 collective-permute-start.1
  136.7 184.9 %all-reduce.19.cloned.1.call-start = ((), (), s32[]{:S(2)}) async-start(), calls=%async_computation.3 | async-start | bytes 1310720 | tf_op jit(solution)/shard_map/psum | solution.py:197
  221.4 15.4 collective-permute-start.3
  241.2 195.3 %all-reduce.21.cloned.1.call-start = ((), (), s32[]{:S(2)}) async-start(), calls=%async_computation.4 | async-start | bytes 1310720 | tf_op jit(solution)/shard_map/psum | solution.py:197
  326.9 15.4 collective-permute-start.5
  354.1 190.4 %all-reduce.23.cloned.1.call-start = ((), (), s32[]{:S(2)}) async-start(), calls=%async_computation.5 | async-start | bytes 1310720 | tf_op jit(solution)/shard_map/psum | solution.py:197
  441.7 15.4 collective-permute-start.7
  461.6 194.2 %all-reduce.25.cloned.1.call-start = ((), (), s32[]{:S(2)}) async-start(), calls=%async_computation.6 | async-start | bytes 1310720 | tf_op jit(solution)/shard_map/psum | solution.py:197
  549.7 15.4 collective-permute-start.9
  576.8 184.4 %all-reduce.27.cloned.1.call-start = ((), (), s32[]{:S(2)}) async-start(), calls=%async_computation.7 | async-start | bytes 1310720 | tf_op jit(solution)/shard_map/psum | solution.py:197
  661.1 15.4 collective-permute-start.11
  680.9 206.8 %all-reduce.29.cloned.1.call-start = ((), (), s32[]{:S(2)}) async-start(), calls=%async_computation.8 | async-start | bytes 1310720 | tf_op jit(solution)/shard_map/psum | solution.py:233
  825.6 183.9 %all-reduce.31.cloned.1.call-start = ((), (), s32[]{:S(2)}) async-start(), calls=%async_computation.9 | async-start | bytes 1310720 | tf_op jit(solution)/shard_map/psum | solution.py:233
  911.8 222.2 %all-reduce.33.cloned.1.call-start = ((), (), s32[]{:S(2)}) async-start(), calls=%async_computation.10 | async-start | bytes 1310720 | tf_op jit(solution)/shard_map/psum | solution.py:233
  1034.7 225.0 %all-reduce.35.cloned.1.call-start = ((), (), s32[]{:S(2)}) async-start(), calls=%async_computation.11 | async-start | bytes 1310720 | tf_op jit(solution)/shard_map/psum | solution.py:233
  1160.1 226.4 %all-reduce.37.cloned.1.call-start = ((), (), s32[]{:S(2)}) async-start(), calls=%async_computation.12 | async-start | bytes 1310720 | tf_op jit(solution)/shard_map/psum | solution.py:233
  1285.9 225.1 %all-reduce.39.cloned.1.call-start = ((), (), s32[]{:S(2)}) async-start(), calls=%async_computation.13 | async-start | bytes 1310720 | tf_op jit(solution)/shard_map/psum | solution.py:233
  1412.7 223.0 %all-reduce.41.cloned.1.call-start = ((), (), s32[]{:S(2)}) async-start(), calls=%async_computation.14 | async-start | bytes 1310720 | tf_op jit(solution)/shard_map/psum | solution.py:233
  1537.3 370.6 %reduce-scatter.2.cloned.1.call-start = ((), (), s32[]{:S(2)}) async-start(), calls=%async_computation.15 | async-start | bytes 11796480 | tf_op jit(solution)/shard_map/reduce_scatter | solution.py:256
  1673.1 34.9 %collective-permute-start.28 = (bf16[128,6656]{0,1:T(8,128)(2,1)S(1)}, bf16[128,6656]{0,1:T(8,128)(2,1)S(1)}, u32[]{:S(2)}, u32[]{:S(2)}) collective-permute-start(bf16[128,6656]{0,1:T(8,128)(2,1)S(1)} %pad_maximum_fusion.17), channel_id=1, source_target_pairs={{0,16},{16,0},{32,48},{48,32},{64,80},{80,64},{96,112},{112,96},{1... | collective-permute-start | bytes 5111816 | tf_op jit(solution)/shard_map/ppermute | solution.py:25
  1707.9 32.6 %collective-permute-start.29 = (bf16[128,6656]{0,1:T(8,128)(2,1)S(1)}, bf16[128,6656]{0,1:T(8,128)(2,1)S(1)}, u32[]{:S(2)}, u32[]{:S(2)}) collective-permute-start(bf16[128,6656]{0,1:T(8,128)(2,1)S(1)} %collective-permute-done.28), channel_id=1, source_target_pairs={{0,32},{16,48},{32,0},{48,16},{64,96},{80,112},{96,64},{112,80},{1... | collective-permute-start | bytes 5111816 | tf_op jit(solution)/shard_map/ppermute | solution.py:25
  1740.5 43.5 %collective-permute-start.30 = (bf16[128,6656]{0,1:T(8,128)(2,1)S(1)}, bf16[128,6656]{0,1:T(8,128)(2,1)S(1)}, u32[]{:S(2)}, u32[]{:S(2)}) collective-permute-start(bf16[128,6656]{0,1:T(8,128)(2,1)S(1)} %collective-permute-done.29), channel_id=1, source_target_pairs={{0,64},{16,80},{32,96},{48,112},{64,0},{80,16},{96,32},{112,48},{1... | collective-permute-start | bytes 5111816 | tf_op jit(solution)/shard_map/ppermute | solution.py:25
  (85 other events, 1709.2 us)
Sparse Core Ops, SparseCore 0:
  39.6 64.7 all-reduce.14
  136.8 79.2 all-reduce.16
  241.3 80.2 all-reduce.18
  354.3 82.1 all-reduce.20
  461.7 82.7 all-reduce.22
  576.9 78.8 all-reduce.24
  681.1 80.0 all-reduce.26
  825.7 61.9 all-reduce.28
  911.9 97.5 all-reduce.30
  1034.8 99.0 all-reduce.32
  1160.2 99.3 all-reduce.34
  1286.0 100.3 all-reduce.36
  1412.8 98.1 all-reduce.38
  1537.4 98.2 all-reduce.40
  1797.5 110.2 reduce-scatter.1
where the time goes:
time: 1940 us; the launch traced here: 1930 us
  waiting for transfers between devices  1570 us (81%)
  local copies, waits for them, and re-layouts  114 us (6%)
  other arithmetic  87.8 us (5%)
  starting transfers between devices  81.1 us (4%)
  matrix products  42.3 us (2%)
  loops' own time  22.8 us (1%)
    psum x7, waiting for transfers between devices, local(): lax.psum(for_sending(normed_grad), 'tensor')  645 us
    psum x7, waiting for transfers between devices, local(): lax.psum(for_sending(partial_value), 'tensor')  542 us
    ppermute x28, waiting for transfers between devices, passed_along(): return lax.ppermute(block, axis, route)  168 us
    reduce_scatter x1, waiting for transfers between devices, local(): lax.psum_scatter(jnp.concatenate([contract_rows(normed_rows, qkv_all), co...  110 us
    ppermute x3, waiting for transfers between devices, from_partner(): return lax.ppermute(value, axis, pairs)  100 us
    ppermute x28, starting transfers between devices, passed_along(): return lax.ppermute(block, axis, route)  68.4 us
    unnamed x128, local copies, waits for them, and re-layouts  42.9 us
  transfers between devices with their start and end apart: 46, of which 46 were waited for; matrix products, arithmetic and copies ran while one was open for 1% of the time, Pallas kernels for 0%

commit v1 on v0

v1 whole, which is shorter than its diff:
```python
import functools
import jax
import jax.numpy as jnp
from jax import lax
from jax.experimental import pallas as pl
from jax.experimental.pallas import tpu as pltpu
from jax.sharding import PartitionSpec as P

HS = 128
EPS = 1e-05
FACTOR = HS ** (-0.5)
F32 = jnp.float32
BF16 = jnp.bfloat16
SHIFTS = (2, 1, 3, 0)
VMEM_LIMIT = 40 * 1024 * 1024


def dot_nn(a, b):
    return lax.dot_general(a, b, (((1,), (0,)), ((), ())), preferred_element_type=F32)


def dot_nt(a, b):
    return lax.dot_general(a, b, (((1,), (1,)), ((), ())), preferred_element_type=F32)


def dot_tn(a, b):
    return lax.dot_general(a, b, (((0,), (0,)), ((), ())), preferred_element_type=F32)


def piece_rows(z, i, half):
    return pl.multiple_of(64 * half + 16 * lax.rem(z + 4 - SHIFTS[i], 4), 16)


def start_weights(d, down, up, held, sems):
    for choice, refs in ((0, down), (1, up)):

        @pl.when(d == choice)
        def _():
            for n, (source, target) in enumerate(zip(refs, held)):
                pltpu.make_async_copy(source, target, sems.at[n]).start()


def wait_weights(n, source, target, sems):
    pltpu.make_async_copy(source, target, sems.at[n]).wait()


def front_kernel(
    last, sc, own, oth, gain, allowed, wd, wu, od, ou, xn_i, qkv_i, prob_i, ctx_i, *refs
):
    if last:
        xn_o, qkv_o, prob_o, ctx_o, w, o, xn, qkv, prob, ctx, wsem, ssem = refs
    else:
        keep, send, xn_o, qkv_o, prob_o, ctx_o, w, o, xn, qkv, prob, ctx, wsem, ssem = refs
    active, d, c, z = sc[0], sc[1], sc[2], sc[3]

    @pl.when(active == 1)
    def _():
        held = [w.at[0], w.at[1], w.at[2]] + ([] if last else [o])
        down = [wd.at[0], wd.at[1], wd.at[2]] + ([] if last else [od])
        up = [wu.at[0], wu.at[1], wu.at[2]] + ([] if last else [ou])
        start_weights(d, down, up, held, wsem)
        g = gain[pl.ds(d, 1), :]
        for ref, half in ((own, c), (oth, 1 - c)):
            for i in range(4):
                x = ref[16 * i : 16 * i + 16, :].astype(F32)
                xc = x - jnp.mean(x, axis=-1, keepdims=True)
                rstd = lax.rsqrt(jnp.mean(xc * xc, axis=-1, keepdims=True) + EPS)
                xn[pl.ds(piece_rows(z, i, half), 16), :] = (xc * rstd * g).astype(BF16)
        copies = [pltpu.make_async_copy(xn, xn_o.at[d], ssem.at[0])]
        copies[0].start()
        for j in range(3):
            wait_weights(j, down[j], held[j], wsem)
            qkv[j] = dot_nn(xn[...], w[j]).astype(BF16)
        copies.append(pltpu.make_async_copy(qkv, qkv_o.at[d], ssem.at[1]))
        copies[1].start()
        mask = allowed[d] > 0.5
        for h in range(3):
            cols = slice(h * HS, h * HS + HS)
            s = dot_nt(qkv[0, :, cols], qkv[1, :, cols]) * FACTOR
            s = jnp.where(mask, s, -1e30)
            e = jnp.exp(s - jnp.max(s, axis=-1, keepdims=True))
            p = e / jnp.sum(e, axis=-1, keepdims=True)
            prob[h] = p
            ctx[:, cols] = dot_nn(p.astype(BF16), qkv[2, :, cols]).astype(BF16)
        copies.append(pltpu.make_async_copy(prob, prob_o.at[d], ssem.at[2]))
        copies.append(pltpu.make_async_copy(ctx, ctx_o.at[d], ssem.at[3]))
        copies[2].start()
        copies[3].start()
        if not last:
            lhs = jnp.concatenate(
                [
                    ctx[pl.ds(pl.multiple_of(64 * (1 - c), 64), 64), :],
                    ctx[pl.ds(pl.multiple_of(64 * c, 64), 64), :],
                ],
                axis=0,
            )
            wait_weights(3, od, o, wsem)
            for n in range(5):
                cols = slice(512 * n, 512 * n + 512)
                part = dot_nt(lhs, o[cols, :]).astype(BF16)
                send[:, cols] = part[:64]
                keep[:, cols] = part[64:]
        for copy in copies:
            copy.wait()


def back_kernel(last, sc, own, oth, wd, wu, od, ou, qkv_i, prob_i, dy_i, dqkv_i, *refs):
    if last:
        dy_o, dqkv_o, w, o, dy, qkv, prob, dqkv, wsem, ssem = refs
    else:
        keep, send, dy_o, dqkv_o, w, o, dy, qkv, prob, dqkv, wsem, ssem = refs
    active, d, c, z = sc[0], sc[1], sc[2], sc[3]

    @pl.when(active == 1)
    def _():
        held = [o] + ([] if last else [w.at[0], w.at[1], w.at[2]])
        down = [od] + ([] if last else [wd.at[0], wd.at[1], wd.at[2]])
        up = [ou] + ([] if last else [wu.at[0], wu.at[1], wu.at[2]])
        loads = [
            pltpu.make_async_copy(qkv_i.at[d], qkv, ssem.at[0]),
            pltpu.make_async_copy(prob_i.at[d], prob, ssem.at[1]),
        ]
        start_weights(d, down[:1], up[:1], held[:1], wsem)
        for load in loads:
            load.start()
        if not last:
            for choice, refs_ in ((0, down), (1, up)):

                @pl.when(d == choice)
                def _():
                    for n in range(1, 4):
                        pltpu.make_async_copy(refs_[n], held[n], wsem.at[n]).start()

        for ref, half in ((own, c), (oth, 1 - c)):
            for i in range(4):
                dy[pl.ds(piece_rows(z, i, half), 16), :] = ref[16 * i : 16 * i + 16, :]
        copies = [pltpu.make_async_copy(dy, dy_o.at[d], ssem.at[2])]
        copies[0].start()
        wait_weights(0, od, o, wsem)
        dctx = dot_nn(dy[...], o[...]).astype(BF16)
        for load in loads:
            load.wait()
        for h in range(3):
            cols = slice(h * HS, h * HS + HS)
            p = prob[h]
            dctx_h = dctx[:, cols]
            dp = dot_nt(dctx_h, qkv[2, :, cols])
            inner = jnp.sum(p * dp, axis=-1, keepdims=True)
            ds = (p * (dp - inner) * FACTOR).astype(BF16)
            dqkv[0, :, cols] = dot_nn(ds, qkv[1, :, cols]).astype(BF16)
            dqkv[1, :, cols] = dot_tn(ds, qkv[0, :, cols]).astype(BF16)
            dqkv[2, :, cols] = dot_tn(p.astype(BF16), dctx_h).astype(BF16)
        copies.append(pltpu.make_async_copy(dqkv, dqkv_o.at[d], ssem.at[3]))
        copies[1].start()
        if not last:
            lhs = []
            for j in range(3):
                lhs.append(
                    jnp.concatenate(
                        [
                            dqkv[j, pl.ds(pl.multiple_of(64 * (1 - c), 64), 64), :],
                            dqkv[j, pl.ds(pl.multiple_of(64 * c, 64), 64), :],
                        ],
                        axis=0,
                    )
                )
            for j in range(3):
                wait_weights(1 + j, wd.at[j], w.at[j], wsem)
            for n in range(5):
                cols = slice(512 * n, 512 * n + 512)
                part = dot_nt(lhs[0], w[0, cols, :])
                part += dot_nt(lhs[1], w[1, cols, :])
                part += dot_nt(lhs[2], w[2, cols, :])
                part = part.astype(BF16)
                send[:, cols] = part[:64]
                keep[:, cols] = part[64:]
        for copy in copies:
            copy.wait()


ANY = pl.BlockSpec(memory_space=pl.ANY)
VM = pl.BlockSpec(memory_space=pltpu.VMEM)
SM = pl.BlockSpec(memory_space=pltpu.SMEM)


def like(a):
    return jax.ShapeDtypeStruct(a.shape, a.dtype)


def spread_like(rows, width):
    return jax.ShapeDtypeStruct((rows, width), BF16)


def front_call(last, sc, own, oth, gain, allowed, weights, state):
    rows, width = own.shape
    wide = weights[2].shape[1]
    xn, qkv, prob, ctx = state
    halves = [] if last else [spread_like(rows, width)] * 2
    first = len(halves)
    return pl.pallas_call(
        functools.partial(front_kernel, last),
        out_shape=halves + [like(a) for a in state],
        in_specs=[SM, VM, VM, VM, VM] + [ANY] * 8,
        out_specs=[VM] * first + [ANY] * 4,
        input_output_aliases={9 + n: first + n for n in range(4)},
        scratch_shapes=[
            pltpu.VMEM((3, width, wide), BF16),
            pltpu.VMEM((width, wide), BF16),
            pltpu.VMEM(xn.shape[1:], BF16),
            pltpu.VMEM(qkv.shape[1:], BF16),
            pltpu.VMEM(prob.shape[1:], F32),
            pltpu.VMEM(ctx.shape[1:], BF16),
            pltpu.SemaphoreType.DMA((4,)),
            pltpu.SemaphoreType.DMA((4,)),
        ],
        compiler_params=pltpu.CompilerParams(vmem_limit_bytes=VMEM_LIMIT),
        cost_estimate=pl.CostEstimate(
            flops=2 * 128 * width * wide * 4, bytes_accessed=8 * width * wide, transcendentals=0
        ),
        name="front",
    )(sc, own, oth, gain, allowed, *weights, *state)


def back_call(last, sc, own, oth, weights, qkv, prob, dy, dqkv):
    rows, width = own.shape
    wide = weights[2].shape[1]
    halves = [] if last else [spread_like(rows, width)] * 2
    first = len(halves)
    return pl.pallas_call(
        functools.partial(back_kernel, last),
        out_shape=halves + [like(dy), like(dqkv)],
        in_specs=[SM, VM, VM] + [ANY] * 8,
        out_specs=[VM] * first + [ANY] * 2,
        input_output_aliases={9: first, 10: first + 1},
        scratch_shapes=[
            pltpu.VMEM((3, width, wide), BF16),
            pltpu.VMEM((width, wide), BF16),
            pltpu.VMEM(dy.shape[1:], BF16),
            pltpu.VMEM(qkv.shape[1:], BF16),
            pltpu.VMEM(prob.shape[1:], F32),
            pltpu.VMEM(dqkv.shape[1:], BF16),
            pltpu.SemaphoreType.DMA((4,)),
            pltpu.SemaphoreType.DMA((4,)),
        ],
        compiler_params=pltpu.CompilerParams(vmem_limit_bytes=VMEM_LIMIT),
        cost_estimate=pl.CostEstimate(
            flops=2 * 128 * width * wide * 4, bytes_accessed=8 * width * wide, transcendentals=0
        ),
        name="back",
    )(sc, own, oth, *weights, qkv, prob, dy, dqkv)


def alloc_kernel(*refs):
    pass


def alloc(shapes):
    return pl.pallas_call(
        alloc_kernel,
        out_shape=[jax.ShapeDtypeStruct(s, t) for s, t in shapes],
        out_specs=[ANY] * len(shapes),
        name="alloc",
    )()


def stage_partner(t, p):
    if t % 2 == 0:
        return p ^ 1
    if t == 3:
        return (7, 2, 1, 4, 3, 6, 5, 0)[p]
    return (3, 2, 1, 0, 7, 6, 5, 4)[p]


AXES = ("pipe", "tensor")


def permute(x, target):
    pairs = []
    for p in range(8):
        for z in range(4):
            for c in range(2):
                tp, tz, tc = target(p, z, c)
                pairs.append((p * 8 + z * 2 + c, tp * 8 + tz * 2 + tc))
    return lax.ppermute(x, AXES, pairs)


def other_core(x):
    return permute(x, lambda p, z, c: (p, z, 1 - c))


def sum_over_tensor(keep, send, z):
    pair = (keep.astype(F32) + other_core(send).astype(F32)).astype(BF16)
    parts = []
    for k in (2, 1, 3):
        block = lax.dynamic_slice_in_dim(pair, 16 * lax.rem(z + k, 4), 16, 0)
        parts.append(permute(block, lambda p, zz, c: (p, (zz + k) % 4, c)))
    own = lax.dynamic_slice_in_dim(pair, 16 * z, 16, 0)
    return own.astype(F32) + parts[0].astype(F32) + parts[1].astype(F32) + parts[2].astype(F32)


def hop_and_spread(block, t):
    pieces = [
        permute(block, lambda p, z, c: (stage_partner(t, p), (z + k) % 4, c)) for k in SHIFTS
    ]
    own = jnp.concatenate(pieces, axis=0)
    return own, other_core(own), pieces[3]


def doc_mask(doc_lengths, row_count):
    doc_ends = jnp.cumsum(doc_lengths)
    places = jnp.arange(row_count, dtype=jnp.int32)
    segment = jnp.sum((places[:, None] >= doc_ends[None, :]).astype(jnp.int32), axis=1)
    return (segment[:, None] == segment[None, :]) & (places[None, :] <= places[:, None])


def in_pieces(x, z, c):
    halves = []
    for half in (c, 1 - c):
        halves.append(
            jnp.concatenate(
                [
                    lax.dynamic_slice_in_dim(x, 64 * half + 16 * lax.rem(z + 4 - k, 4), 16, 0)
                    for k in SHIFTS
                ],
                axis=0,
            )
        )
    return halves[0], halves[1], halves[0][48:]


def mean(x):
    return jnp.mean(x, axis=-1, keepdims=True)


def local(inputs, cotangent, lengths, down_qkv, down_out, down_gain, up_qkv, up_out, up_gain):
    place = lax.axis_index("pipe")
    tensor = lax.axis_index("tensor")
    z, c = tensor // 2, tensor % 2
    rows, width = inputs.shape[1], inputs.shape[2]
    wide = down_out.shape[2]
    weights = (
        jnp.transpose(down_qkv[0], (1, 0, 2)),
        jnp.transpose(up_qkv[0], (1, 0, 2)),
        down_out[0],
        up_out[0],
    )
    gain = jnp.concatenate([down_gain, up_gain], axis=0).astype(F32)
    allowed = jnp.stack([doc_mask(lengths[r, 0], rows) for r in range(2)]).astype(F32)

    def scalars(is_down, is_up):
        active = (is_down | is_up).astype(jnp.int32)
        return jnp.stack([active, is_up.astype(jnp.int32), c, z]).astype(jnp.int32)

    state = alloc(
        [
            ((2, rows, width), BF16),
            ((2, 3, rows, wide), BF16),
            ((2, 3, rows, rows), F32),
            ((2, rows, wide), BF16),
        ]
    )
    dy_state, dqkv_state = alloc([((2, rows, width), BF16), ((2, 3, rows, wide), BF16)])

    own, oth, block = in_pieces(jnp.where(place == 0, inputs[0], inputs[1]), z, c)
    kept = [block, block]
    for t in range(8):
        is_down, is_up = place == t, place == 7 - t
        sc = scalars(is_down, is_up)
        kept = [jnp.where(is_down, block, kept[0]), jnp.where(is_up, block, kept[1])]
        if t < 7:
            keep, send, *state = front_call(False, sc, own, oth, gain, allowed, weights, state)
            total = sum_over_tensor(keep, send, z)
            result = (block.astype(F32) + total).astype(BF16)
            own, oth, block = hop_and_spread(result, t)
        else:
            state = front_call(True, sc, own, oth, gain, allowed, weights, state)
    xn, qkv, prob, ctx = state

    x = jnp.stack(kept).astype(F32)
    xc = x - mean(x)
    rstd = lax.rsqrt(mean(xc * xc) + EPS)
    xhat = xc * rstd

    own, oth, block = in_pieces(jnp.where(place == 7, cotangent[0], cotangent[1]), z, c)
    for t in range(8):
        is_down, is_up = place == 7 - t, place == t
        sc = scalars(is_down, is_up)
        if t < 7:
            keep, send, dy_state, dqkv_state = back_call(
                False, sc, own, oth, weights, qkv, prob, dy_state, dqkv_state
            )
            dxn = sum_over_tensor(keep, send, z)
            xhat_d = jnp.where(is_down, xhat[0], xhat[1])
            rstd_d = jnp.where(is_down, rstd[0], rstd[1])
            gr = dxn * jnp.where(is_down, gain[0:1], gain[1:2])
            change = rstd_d * (gr - mean(gr) - xhat_d * mean(gr * xhat_d))
            result = (block.astype(F32) + change).astype(BF16)
            own, oth, block = hop_and_spread(result, t)
        else:
            dy_state, dqkv_state = back_call(
                True, sc, own, oth, weights, qkv, prob, dy_state, dqkv_state
            )

    b = lax.axis_index("dp")
    half = width // 2

    def feature_half(a, which):
        return lax.dynamic_slice_in_dim(a, which * half, half, axis=-1)

    def pack(d, which):
        return jnp.concatenate(
            [
                feature_half(xn[d], which),
                feature_half(dy_state[d], which),
                ctx[d],
                dqkv_state[d, 0],
                dqkv_state[d, 1],
                dqkv_state[d, 2],
            ],
            axis=1,
        )

    def mirror(a, flip):
        pairs = [(p * 2 + bb, (7 - p) * 2 + (bb ^ flip)) for bb in range(2) for p in range(8)]
        return lax.ppermute(a, ("pipe", "dp"), pairs)

    packs = [
        pack(0, b),
        lax.ppermute(pack(0, 1 - b), "dp", [(0, 1), (1, 0)]),
        mirror(pack(1, b), 0),
        mirror(pack(1, 1 - b), 1),
    ]
    every = jnp.concatenate(packs, axis=0)
    xn_all = every[:, :half]
    dy_all = every[:, half : 2 * half]
    ctx_all = every[:, 2 * half : 2 * half + wide]
    dqkv_all = every[:, 2 * half + wide :]
    grad_qkv = dot_tn(xn_all, dqkv_all) * 0.5
    grad_out = dot_tn(dy_all, ctx_all) * 0.5
    return grad_qkv.reshape(1, half, 3, wide), grad_out.reshape(1, half, wide)


def solution(mesh):
    placed = (
        P(None, "dp", None),
        P(None, "dp", None),
        P(None, "dp", None),
        P("pipe", None, None, "tensor"),
        P("pipe", None, "tensor"),
        P("pipe", None),
        P("pipe", None, None, "tensor"),
        P("pipe", None, "tensor"),
        P("pipe", None),
    )
    return jax.shard_map(
        local,
        mesh=mesh,
        in_specs=placed,
        out_specs=(P("pipe", "dp", None, "tensor"), P("pipe", "dp", "tensor")),
        check_vma=False,
    )
```

time: 1940 us -> 602 us (0.31)
  waiting for transfers between devices: 1570 us -> 211 us
  starting transfers between devices: 81.1 us -> 244 us
  other arithmetic: 87.8 us -> 15.8 us
  matrix products: 42.3 us -> 7.77 us
  Pallas kernels: 0 us -> 31.9 us
  local copies, waits for them, and re-layouts: 114 us -> 83.9 us
  loops' own time: 22.8 us -> 0 us
    psum x14 -> x0, waiting for transfers between devices: 1190 us -> none  [the longest x7 645 us: local(): lax.psum(for_sending(normed_grad), 'tensor')]
    ppermute x31 -> x129, starting transfers between devices: 78.9 us -> 244 us  [the longest x126 239 us: permute(): return lax.ppermute(x, AXES, pairs)]
    reduce_scatter x1 -> x0, waiting for transfers between devices: 110 us -> none  [local(): lax.psum_scatter(jnp.concatenate([contract_rows(normed_rows, qkv_all), co...]
    ppermute x31 -> x129, waiting for transfers between devices: 268 us -> 211 us  [the longest x126 148 us: permute(): return lax.ppermute(x, AXES, pairs)]
    dot_general x23 -> x2, matrix products: 42.3 us -> 7.77 us  [dot_tn(): lax.dot_general(a, b, (((0,), (0,)), ((), ())), preferred_element_type=F32)]
    cond x22 -> x0, local copies, waits for them, and re-layouts: 33.4 us -> none  [the longest x9 17.9 us: local(): lax.switch(section_role, back_branches, section_input, chosen)]
    pallas_call x0 -> x18, Pallas kernels: none -> 31.9 us  [the longest x8 19 us: front_call(): pl.pallas_call(functools.partial(front_kernel, last), out_shape=halves +...]
    unnamed x128 -> x213, local copies, waits for them, and re-layouts: 42.9 us -> 74.6 us
  transfers between devices with their start and end apart: 46 -> 129, of which waited for: 46 -> 89; matrix products, arithmetic and copies ran while one was open for 1% -> 2% of each run, Pallas kernels for 0% -> 0%
where the time goes in v1:
time: 602 us; the launch traced here: 596 us
  starting transfers between devices  244 us (41%)
  waiting for transfers between devices  211 us (35%)
  local copies, waits for them, and re-layouts  83.9 us (14%)
  Pallas kernels  31.9 us (5%)
  other arithmetic  15.8 us (3%)
  matrix products  7.77 us (1%)
    ppermute x126, starting transfers between devices, permute(): return lax.ppermute(x, AXES, pairs)  239 us
    ppermute x126, waiting for transfers between devices, permute(): return lax.ppermute(x, AXES, pairs)  148 us
    unnamed x213, local copies, waits for them, and re-layouts  74.6 us
    ppermute x2, waiting for transfers between devices, mirror(): return lax.ppermute(a, ('pipe', 'dp'), pairs)  62.9 us
    pallas_call x8, Pallas kernels, front_call(): pl.pallas_call(functools.partial(front_kernel, last), out_shape=halves +...  19 us
    pallas_call x8, Pallas kernels, back_call(): pl.pallas_call(functools.partial(back_kernel, last), out_shape=halves + [...  12.9 us
  transfers between devices with their start and end apart: 129, of which 89 were waited for; matrix products, arithmetic and copies ran while one was open for 2% of the time, Pallas kernels for 0%

profile of v1, /device:TPU:1, one launch (start us, length us, event | category | flops | bytes accessed | tf_op | source)
XLA Modules:
  0.0 596.3 jit_solution(9772971133581984583)
XLA Ops:
  11.3 6.7 %front.8 = (bf16[64,2560]{1,0:T(8,128)(2,1)S(1)}, bf16[64,2560]{1,0:T(8,128)(2,1)}, bf16[2,128,2560]{2,1,0:T(8,128)(2,1)S(1)}, bf16[2,3,128,384]{3,2,1,0:T(8,128...) custom-call(s32[4]{0:T(128)S(1)} %add_add_fusion.1.sc, ...), custom_call_target="tpu_custom_call", output_to_operand_aliasing={{2}: (9, {}), {3}: (10, {}), {4}: (11, {}), {5}: (12, {})} | custom-call | flops 1006632960 | bytes 7864320 | tf_op jit(solution)/shard_map/front/pallas_call | solution.py:200
  26.1 3.7 collective-permute-start.1
  36.2 3.7 collective-permute-start.7
  68.6 4.7 collective-permute-start.16
  138.5 3.9 collective-permute-start.32
  143.1 12.3 %collective-permute-start.33 = (bf16[16,2560]{1,0:T(8,128)(2,1)S(1)}, bf16[16,2560]{1,0:T(8,128)(2,1)S(1)}, u32[]{:S(2)}, u32[]{:S(2)}) collective-permute-start(bf16[16,2560]{1,0:T(8,128)(2,1)S(1)} %add_convert_fusion.17), channel_id=1, source_target_pairs={{0,116},{2,118},{4,120},{6,122},{8,124},{10,126},{12,112},{14,114}... | collective-permute-start | bytes 245768 | tf_op jit(solution)/shard_map/ppermute | solution.py:284
  221.1 17.6 %collective-permute-start.50 = (bf16[16,2560]{1,0:T(8,128)(2,1)S(1)}, bf16[16,2560]{1,0:T(8,128)(2,1)S(1)}, u32[]{:S(2)}, u32[]{:S(2)}) collective-permute-start(bf16[16,2560]{1,0:T(8,128)(2,1)S(1)} %add_convert_fusion.15), channel_id=1, source_target_pairs={{0,56},{2,58},{4,60},{6,62},{8,48},{10,50},{12,52},{14,54},{16,40}... | collective-permute-start | bytes 245768 | tf_op jit(solution)/shard_map/ppermute | solution.py:284
  238.8 4.0 collective-permute-start.51
  265.8 10.3 %collective-permute-start.58 = (bf16[16,2560]{1,0:T(8,128)(2,1)S(1)}, bf16[16,2560]{1,0:T(8,128)(2,1)S(1)}, u32[]{:S(2)}, u32[]{:S(2)}) collective-permute-start(bf16[16,2560]{1,0:T(8,128)(2,1)S(1)} %add_convert_fusion.14), channel_id=1, source_target_pairs={{0,24},{2,26},{4,28},{6,30},{8,16},{10,18},{12,20},{14,22},{16,8},... | collective-permute-start | bytes 245768 | tf_op jit(solution)/shard_map/ppermute | solution.py:284
  278.7 5.0 collective-permute-done.59
  289.3 5.8 front.15
  296.1 6.1 %back.8 = (bf16[64,2560]{1,0:T(8,128)(2,1)S(1)}, bf16[64,2560]{1,0:T(8,128)(2,1)S(1)}, bf16[2,128,2560]{2,1,0:T(8,128)(2,1)S(1)}, bf16[2,3,128,384]{3,2,1,0:T(8,128)(2,1)S(1)}) custom-call(s32[4]{0:T(128)S(1)} %add_add_fusion.sc, bf16[64,2560]{1,0:T(8,128)(2,1)S(1)} %get-tuple-element.297.own, ...), custom_call_target="tpu_custom_call", output_to_operand_aliasing={{2}: (9, {}), {3}: (10, {})} | custom-call | flops 1006632960 | bytes 7864320 | tf_op jit(solution)/shard_map/back/pallas_call | solution.py:229
  333.7 5.0 collective-permute-start.79
  359.0 5.7 collective-permute-start.86
  387.3 3.9 collective-permute-start.97
  394.7 4.0 collective-permute-done.96
  437.5 16.6 %collective-permute-start.113 = (bf16[16,2560]{1,0:T(8,128)(2,1)S(1)}, bf16[16,2560]{1,0:T(8,128)(2,1)S(1)}, u32[]{:S(2)}, u32[]{:S(2)}) collective-permute-start(bf16[16,2560]{1,0:T(8,128)(2,1)S(1)} %fusion.23), channel_id=1, source_target_pairs={{0,56},{2,58},{4,60},{6,62},{8,48},{10,50},{12,52},{14,54},{16,40}... | collective-permute-start | bytes 245768 | tf_op jit(solution)/shard_map/ppermute | solution.py:284
  481.4 10.4 %collective-permute-start.121 = (bf16[16,2560]{1,0:T(8,128)(2,1)S(1)}, bf16[16,2560]{1,0:T(8,128)(2,1)S(1)}, u32[]{:S(2)}, u32[]{:S(2)}) collective-permute-start(bf16[16,2560]{1,0:T(8,128)(2,1)S(1)} %fusion.18), channel_id=1, source_target_pairs={{0,24},{2,26},{4,28},{6,30},{8,16},{10,18},{12,20},{14,22},{16,8},... | collective-permute-start | bytes 245768 | tf_op jit(solution)/shard_map/ppermute | solution.py:284
  494.5 5.5 collective-permute-done.122
  511.2 4.3 collective-permute-start.128
  516.6 53.5 %collective-permute-done.128 = bf16[128,4096]{1,0:T(8,128)(2,1)S(1)} collective-permute-done((bf16[128,4096]{1,0:T(8,128)(2,1)S(1)}, bf16[128,4096]{1,0:T(8,128)(2,1)S(1)}, u32[]{:S(2)}, u32[]{:S(2)}) %collective-permute-start.128) | collective-permute-done | bytes 1048608 | tf_op jit(solution)/shard_map/ppermute | solution.py:425
  570.1 9.5 %collective-permute-done.127 = bf16[128,4096]{1,0:T(8,128)(2,1)S(1)} collective-permute-done((bf16[128,4096]{1,0:T(8,128)(2,1)S(1)}, bf16[128,4096]{1,0:T(8,128)(2,1)S(1)}, u32[]{:S(2)}, u32[]{:S(2)}) %collective-permute-start.127) | collective-permute-done | bytes 1048608 | tf_op jit(solution)/shard_map/ppermute | solution.py:425
  580.6 4.3 convolution_multiply_fusion
  584.9 7.7 %copy.60 = f32[1,1280,3,384]{3,1,2,0:T(8,128)} copy(f32[1,1280,3,384]{1,3,2,0:T(8,128)} %bitcast.278) | data formatting | bytes 11796480
  (581 shorter events, 379.9 us)
Async XLA Ops:
  36.2 10.2 %collective-permute-start.7 = (bf16[16,2560]{1,0:T(8,128)(2,1)S(1)}, bf16[16,2560]{1,0:T(8,128)(2,1)S(1)}, u32[]{:S(2)}, u32[]{:S(2)}) collective-permute-start(bf16[16,2560]{1,0:T(8,128)(2,1)S(1)} %add_convert_fusion.20), channel_id=1, source_target_pairs={{0,28},{2,30},{4,16},{6,18},{8,20},{10,22},{12,24},{14,26},{16,12}... | collective-permute-start | bytes 245768 | tf_op jit(solution)/shard_map/ppermute | solution.py:284
  68.5 8.6 %collective-permute-start.14 = (bf16[16,2560]{1,0:T(8,128)(2,1)S(1)}, bf16[16,2560]{1,0:T(8,128)(2,1)S(1)}, u32[]{:S(2)}, u32[]{:S(2)}) collective-permute-start(bf16[16,2560]{1,0:T(8,128)(2,1)S(1)} %add_convert_fusion.19), channel_id=1, source_target_pairs={{0,56},{2,58},{4,60},{6,62},{8,48},{10,50},{12,52},{14,54},{16,40}... | collective-permute-start | bytes 245768 | tf_op jit(solution)/shard_map/ppermute | solution.py:284
  68.6 12.2 %collective-permute-start.16 = (bf16[16,2560]{1,0:T(8,128)(2,1)S(1)}, bf16[16,2560]{1,0:T(8,128)(2,1)S(1)}, u32[]{:S(2)}, u32[]{:S(2)}) collective-permute-start(bf16[16,2560]{1,0:T(8,128)(2,1)S(1)} %add_convert_fusion.19), channel_id=1, source_target_pairs={{0,60},{2,62},{4,48},{6,50},{8,52},{10,54},{12,56},{14,58},{16,44}... | collective-permute-start | bytes 245768 | tf_op jit(solution)/shard_map/ppermute | solution.py:284
  73.6 7.9 %collective-permute-start.13 = (bf16[16,2560]{1,0:T(8,128)(2,1)S(1)}, bf16[16,2560]{1,0:T(8,128)(2,1)S(1)}, u32[]{:S(2)}, u32[]{:S(2)}) collective-permute-start(bf16[16,2560]{1,0:T(8,128)(2,1)S(1)} %add_convert_fusion.19), channel_id=1, source_target_pairs={{0,48},{2,50},{4,52},{6,54},{8,56},{10,58},{12,60},{14,62},{16,32}... | collective-permute-start | bytes 245768 | tf_op jit(solution)/shard_map/ppermute | solution.py:284
  138.5 17.1 %collective-permute-start.32 = (bf16[16,2560]{1,0:T(8,128)(2,1)S(1)}, bf16[16,2560]{1,0:T(8,128)(2,1)S(1)}, u32[]{:S(2)}, u32[]{:S(2)}) collective-permute-start(bf16[16,2560]{1,0:T(8,128)(2,1)S(1)} %add_convert_fusion.17), channel_id=1, source_target_pairs={{0,120},{2,122},{4,124},{6,126},{8,112},{10,114},{12,116},{14,118}... | collective-permute-start | bytes 245768 | tf_op jit(solution)/shard_map/ppermute | solution.py:284
  142.3 17.5 %collective-permute-start.34 = (bf16[16,2560]{1,0:T(8,128)(2,1)S(1)}, bf16[16,2560]{1,0:T(8,128)(2,1)S(1)}, u32[]{:S(2)}, u32[]{:S(2)}) collective-permute-start(bf16[16,2560]{1,0:T(8,128)(2,1)S(1)} %add_convert_fusion.17), channel_id=1, source_target_pairs={{0,124},{2,126},{4,112},{6,114},{8,116},{10,118},{12,120},{14,122}... | collective-permute-start | bytes 245768 | tf_op jit(solution)/shard_map/ppermute | solution.py:284
  143.1 16.1 %collective-permute-start.33 = (bf16[16,2560]{1,0:T(8,128)(2,1)S(1)}, bf16[16,2560]{1,0:T(8,128)(2,1)S(1)}, u32[]{:S(2)}, u32[]{:S(2)}) collective-permute-start(bf16[16,2560]{1,0:T(8,128)(2,1)S(1)} %add_convert_fusion.17), channel_id=1, source_target_pairs={{0,116},{2,118},{4,120},{6,122},{8,124},{10,126},{12,112},{14,114}... | collective-permute-start | bytes 245768 | tf_op jit(solution)/shard_map/ppermute | solution.py:284
  185.8 8.9 %collective-permute-start.43 = (bf16[16,2560]{1,0:T(8,128)(2,1)S(1)}, bf16[16,2560]{1,0:T(8,128)(2,1)S(1)}, u32[]{:S(2)}, u32[]{:S(2)}) collective-permute-start(bf16[16,2560]{1,0:T(8,128)(2,1)S(1)} %add_convert_fusion.16), channel_id=1, source_target_pairs={{0,28},{2,30},{4,16},{6,18},{8,20},{10,22},{12,24},{14,26},{16,12}... | collective-permute-start | bytes 245768 | tf_op jit(solution)/shard_map/ppermute | solution.py:284
  188.3 7.7 %collective-permute-start.40 = (bf16[16,2560]{1,0:T(8,128)(2,1)S(1)}, bf16[16,2560]{1,0:T(8,128)(2,1)S(1)}, u32[]{:S(2)}, u32[]{:S(2)}) collective-permute-start(bf16[16,2560]{1,0:T(8,128)(2,1)S(1)} %add_convert_fusion.16), channel_id=1, source_target_pairs={{0,16},{2,18},{4,20},{6,22},{8,24},{10,26},{12,28},{14,30},{16,0},... | collective-permute-start | bytes 245768 | tf_op jit(solution)/shard_map/ppermute | solution.py:284
  221.1 21.6 %collective-permute-start.50 = (bf16[16,2560]{1,0:T(8,128)(2,1)S(1)}, bf16[16,2560]{1,0:T(8,128)(2,1)S(1)}, u32[]{:S(2)}, u32[]{:S(2)}) collective-permute-start(bf16[16,2560]{1,0:T(8,128)(2,1)S(1)} %add_convert_fusion.15), channel_id=1, source_target_pairs={{0,56},{2,58},{4,60},{6,62},{8,48},{10,50},{12,52},{14,54},{16,40}... | collective-permute-start | bytes 245768 | tf_op jit(solution)/shard_map/ppermute | solution.py:284
  265.8 12.8 %collective-permute-start.58 = (bf16[16,2560]{1,0:T(8,128)(2,1)S(1)}, bf16[16,2560]{1,0:T(8,128)(2,1)S(1)}, u32[]{:S(2)}, u32[]{:S(2)}) collective-permute-start(bf16[16,2560]{1,0:T(8,128)(2,1)S(1)} %add_convert_fusion.14), channel_id=1, source_target_pairs={{0,24},{2,26},{4,28},{6,30},{8,16},{10,18},{12,20},{14,22},{16,8},... | collective-permute-start | bytes 245768 | tf_op jit(solution)/shard_map/ppermute | solution.py:284
  311.1 9.2 %collective-permute-start.70 = (bf16[16,2560]{1,0:T(8,128)(2,1)S(1)}, bf16[16,2560]{1,0:T(8,128)(2,1)S(1)}, u32[]{:S(2)}, u32[]{:S(2)}) collective-permute-start(bf16[16,2560]{1,0:T(8,128)(2,1)S(1)} %fusion.48), channel_id=1, source_target_pairs={{0,28},{2,30},{4,16},{6,18},{8,20},{10,22},{12,24},{14,26},{16,12}... | collective-permute-start | bytes 245768 | tf_op jit(solution)/shard_map/ppermute | solution.py:284
  333.6 8.5 %collective-permute-start.77 = (bf16[16,2560]{1,0:T(8,128)(2,1)S(1)}, bf16[16,2560]{1,0:T(8,128)(2,1)S(1)}, u32[]{:S(2)}, u32[]{:S(2)}) collective-permute-start(bf16[16,2560]{1,0:T(8,128)(2,1)S(1)} %fusion.43), channel_id=1, source_target_pairs={{0,56},{2,58},{4,60},{6,62},{8,48},{10,50},{12,52},{14,54},{16,40}... | collective-permute-start | bytes 245768 | tf_op jit(solution)/shard_map/ppermute | solution.py:284
  333.7 11.6 %collective-permute-start.79 = (bf16[16,2560]{1,0:T(8,128)(2,1)S(1)}, bf16[16,2560]{1,0:T(8,128)(2,1)S(1)}, u32[]{:S(2)}, u32[]{:S(2)}) collective-permute-start(bf16[16,2560]{1,0:T(8,128)(2,1)S(1)} %fusion.43), channel_id=1, source_target_pairs={{0,60},{2,62},{4,48},{6,50},{8,52},{10,54},{12,56},{14,58},{16,44}... | collective-permute-start | bytes 245768 | tf_op jit(solution)/shard_map/ppermute | solution.py:284
  359.0 8.1 %collective-permute-start.86 = (bf16[16,2560]{1,0:T(8,128)(2,1)S(1)}, bf16[16,2560]{1,0:T(8,128)(2,1)S(1)}, u32[]{:S(2)}, u32[]{:S(2)}) collective-permute-start(bf16[16,2560]{1,0:T(8,128)(2,1)S(1)} %fusion.38), channel_id=1, source_target_pairs={{0,24},{2,26},{4,28},{6,30},{8,16},{10,18},{12,20},{14,22},{16,8},... | collective-permute-start | bytes 245768 | tf_op jit(solution)/shard_map/ppermute | solution.py:284
  385.3 9.4 %collective-permute-start.95 = (bf16[16,2560]{1,0:T(8,128)(2,1)S(1)}, bf16[16,2560]{1,0:T(8,128)(2,1)S(1)}, u32[]{:S(2)}, u32[]{:S(2)}) collective-permute-start(bf16[16,2560]{1,0:T(8,128)(2,1)S(1)} %fusion.33), channel_id=1, source_target_pairs={{0,120},{2,122},{4,124},{6,126},{8,112},{10,114},{12,116},{14,118}... | collective-permute-start | bytes 245768 | tf_op jit(solution)/shard_map/ppermute | solution.py:284
  387.3 11.5 %collective-permute-start.97 = (bf16[16,2560]{1,0:T(8,128)(2,1)S(1)}, bf16[16,2560]{1,0:T(8,128)(2,1)S(1)}, u32[]{:S(2)}, u32[]{:S(2)}) collective-permute-start(bf16[16,2560]{1,0:T(8,128)(2,1)S(1)} %fusion.33), channel_id=1, source_target_pairs={{0,124},{2,126},{4,112},{6,114},{8,116},{10,118},{12,120},{14,122}... | collective-permute-start | bytes 245768 | tf_op jit(solution)/shard_map/ppermute | solution.py:284
  437.5 20.2 %collective-permute-start.113 = (bf16[16,2560]{1,0:T(8,128)(2,1)S(1)}, bf16[16,2560]{1,0:T(8,128)(2,1)S(1)}, u32[]{:S(2)}, u32[]{:S(2)}) collective-permute-start(bf16[16,2560]{1,0:T(8,128)(2,1)S(1)} %fusion.23), channel_id=1, source_target_pairs={{0,56},{2,58},{4,60},{6,62},{8,48},{10,50},{12,52},{14,54},{16,40}... | collective-permute-start | bytes 245768 | tf_op jit(solution)/shard_map/ppermute | solution.py:284
  481.4 13.0 %collective-permute-start.121 = (bf16[16,2560]{1,0:T(8,128)(2,1)S(1)}, bf16[16,2560]{1,0:T(8,128)(2,1)S(1)}, u32[]{:S(2)}, u32[]{:S(2)}) collective-permute-start(bf16[16,2560]{1,0:T(8,128)(2,1)S(1)} %fusion.18), channel_id=1, source_target_pairs={{0,24},{2,26},{4,28},{6,30},{8,16},{10,18},{12,20},{14,22},{16,8},... | collective-permute-start | bytes 245768 | tf_op jit(solution)/shard_map/ppermute | solution.py:284
  491.9 8.0 %collective-permute-start.124 = (bf16[16,2560]{1,0:T(8,128)(2,1)S(1)}, bf16[16,2560]{1,0:T(8,128)(2,1)S(1)}, u32[]{:S(2)}, u32[]{:S(2)}) collective-permute-start(bf16[16,2560]{1,0:T(8,128)(2,1)S(1)} %fusion.18), channel_id=1, source_target_pairs={{0,16},{2,18},{4,20},{6,22},{8,24},{10,26},{12,28},{14,30},{16,0},... | collective-permute-start | bytes 245768 | tf_op jit(solution)/shard_map/ppermute | solution.py:284
  492.0 7.9 %collective-permute-start.123 = (bf16[16,2560]{1,0:T(8,128)(2,1)S(1)}, bf16[16,2560]{1,0:T(8,128)(2,1)S(1)}, u32[]{:S(2)}, u32[]{:S(2)}) collective-permute-start(bf16[16,2560]{1,0:T(8,128)(2,1)S(1)} %fusion.18), channel_id=1, source_target_pairs={{0,28},{2,30},{4,16},{6,18},{8,20},{10,22},{12,24},{14,26},{16,12}... | collective-permute-start | bytes 245768 | tf_op jit(solution)/shard_map/ppermute | solution.py:284
  511.2 58.9 %collective-permute-start.128 = (bf16[128,4096]{1,0:T(8,128)(2,1)S(1)}, bf16[128,4096]{1,0:T(8,128)(2,1)S(1)}, u32[]{:S(2)}, u32[]{:S(2)}) collective-permute-start(bf16[128,4096]{1,0:T(8,128)(2,1)S(1)} %constant_dynamic-update-slice_fusion.68), channel_id=1, source_target_pairs={{0,113},{16,97},{32,81},{48,65},{64,49},{80,33},{96,17},{112,1},{1... | collective-permute-start | bytes 3145736 | tf_op jit(solution)/shard_map/ppermute | solution.py:425
  515.5 54.6 %collective-permute-start.126 = (bf16[128,4096]{1,0:T(8,128)(2,1)S(1)}, bf16[128,4096]{1,0:T(8,128)(2,1)S(1)}, u32[]{:S(2)}, u32[]{:S(2)}) collective-permute-start(bf16[128,4096]{1,0:T(8,128)(2,1)S(1)} %get-tuple-element.235), channel_id=1, source_target_pairs={{0,1},{1,0},{2,3},{3,2},{4,5},{5,4},{6,7},{7,6},{8,9},{9,8},{10,11... | collective-permute-start | bytes 3145736 | tf_op jit(solution)/shard_map/ppermute | solution.py:429
  516.0 63.5 %collective-permute-start.127 = (bf16[128,4096]{1,0:T(8,128)(2,1)S(1)}, bf16[128,4096]{1,0:T(8,128)(2,1)S(1)}, u32[]{:S(2)}, u32[]{:S(2)}) collective-permute-start(bf16[128,4096]{1,0:T(8,128)(2,1)S(1)} %get-tuple-element.230), channel_id=1, source_target_pairs={{0,112},{16,96},{32,80},{48,64},{64,48},{80,32},{96,16},{112,0},{1... | collective-permute-start | bytes 3145736 | tf_op jit(solution)/shard_map/ppermute | solution.py:425
  (186 other events, 1770.8 us)

commit v2 on v1

--- a/solution.py
+++ b/solution.py
@@ -11,8 +11,9 @@
 FACTOR = HS ** (-0.5)
 F32 = jnp.float32
 BF16 = jnp.bfloat16
-SHIFTS = (2, 1, 3, 0)
-VMEM_LIMIT = 40 * 1024 * 1024
+SHIFTS = (0, 1, 3, 2)
+WEIGHT_PARTS = 2
+VMEM_LIMIT = 52 * 1024 * 1024
 
 
 def dot_nn(a, b):
@@ -37,7 +38,10 @@
         @pl.when(d == choice)
         def _():
             for n, (source, target) in enumerate(zip(refs, held)):
-                pltpu.make_async_copy(source, target, sems.at[n]).start()
+                size = source.shape[0] // WEIGHT_PARTS
+                for m in range(WEIGHT_PARTS):
+                    part = pl.ds(m * size, size)
+                    pltpu.make_async_copy(source.at[part], target.at[part], sems.at[n]).start()
 
 
 def wait_weights(n, source, target, sems):
@@ -81,7 +85,10 @@
             e = jnp.exp(s - jnp.max(s, axis=-1, keepdims=True))
             p = e / jnp.sum(e, axis=-1, keepdims=True)
             prob[h] = p
-            ctx[:, cols] = dot_nn(p.astype(BF16), qkv[2, :, cols]).astype(BF16)
+            ctx_h = dot_nn(p.astype(BF16), qkv[2, :, cols]).astype(BF16)
+            for side in range(2):
+                at = side * 3 * HS + h * HS
+                ctx[:, at : at + HS] = ctx_h[64 * side : 64 * side + 64]
         copies.append(pltpu.make_async_copy(prob, prob_o.at[d], ssem.at[2]))
         copies.append(pltpu.make_async_copy(ctx, ctx_o.at[d], ssem.at[3]))
         copies[2].start()
@@ -89,8 +96,8 @@
         if not last:
             lhs = jnp.concatenate(
                 [
-                    ctx[pl.ds(pl.multiple_of(64 * (1 - c), 64), 64), :],
-                    ctx[pl.ds(pl.multiple_of(64 * c, 64), 64), :],
+                    ctx[:, pl.ds(pl.multiple_of(side * 3 * HS, HS), 3 * HS)]
+                    for side in (1 - c, c)
                 ],
                 axis=0,
             )
@@ -120,17 +127,9 @@
             pltpu.make_async_copy(qkv_i.at[d], qkv, ssem.at[0]),
             pltpu.make_async_copy(prob_i.at[d], prob, ssem.at[1]),
         ]
-        start_weights(d, down[:1], up[:1], held[:1], wsem)
+        start_weights(d, down, up, held, wsem)
         for load in loads:
             load.start()
-        if not last:
-            for choice, refs_ in ((0, down), (1, up)):
-
-                @pl.when(d == choice)
-                def _():
-                    for n in range(1, 4):
-                        pltpu.make_async_copy(refs_[n], held[n], wsem.at[n]).start()
-
         for ref, half in ((own, c), (oth, 1 - c)):
             for i in range(4):
                 dy[pl.ds(piece_rows(z, i, half), 16), :] = ref[16 * i : 16 * i + 16, :]
@@ -147,9 +146,15 @@
             dp = dot_nt(dctx_h, qkv[2, :, cols])
             inner = jnp.sum(p * dp, axis=-1, keepdims=True)
             ds = (p * (dp - inner) * FACTOR).astype(BF16)
-            dqkv[0, :, cols] = dot_nn(ds, qkv[1, :, cols]).astype(BF16)
-            dqkv[1, :, cols] = dot_tn(ds, qkv[0, :, cols]).astype(BF16)
-            dqkv[2, :, cols] = dot_tn(p.astype(BF16), dctx_h).astype(BF16)
+            grads = (
+                dot_nn(ds, qkv[1, :, cols]).astype(BF16),
+                dot_tn(ds, qkv[0, :, cols]).astype(BF16),
+                dot_tn(p.astype(BF16), dctx_h).astype(BF16),
+            )
+            for j in range(3):
+                for side in range(2):
+                    at = (side * 3 + j) * 3 * HS + h * HS
+                    dqkv[:, at : at + HS] = grads[j][64 * side : 64 * side + 64]
         copies.append(pltpu.make_async_copy(dqkv, dqkv_o.at[d], ssem.at[3]))
         copies[1].start()
         if not last:
@@ -158,8 +163,8 @@
                 lhs.append(
                     jnp.concatenate(
                         [
-                            dqkv[j, pl.ds(pl.multiple_of(64 * (1 - c), 64), 64), :],
-                            dqkv[j, pl.ds(pl.multiple_of(64 * c, 64), 64), :],
+                            dqkv[:, pl.ds(pl.multiple_of((side * 3 + j) * 3 * HS, HS), 3 * HS)]
+                            for side in (1 - c, c)
                         ],
                         axis=0,
                     )
@@ -178,7 +183,7 @@
             copy.wait()
 
 
-ANY = pl.BlockSpec(memory_space=pl.ANY)
+ANY = pl.BlockSpec(memory_space=pltpu.HBM)
 VM = pl.BlockSpec(memory_space=pltpu.VMEM)
 SM = pl.BlockSpec(memory_space=pltpu.SMEM)
 
@@ -303,7 +308,70 @@
         permute(block, lambda p, z, c: (stage_partner(t, p), (z + k) % 4, c)) for k in SHIFTS
     ]
     own = jnp.concatenate(pieces, axis=0)
-    return own, other_core(own), pieces[3]
+    return own, other_core(own), pieces[0]
+
+
+def mirror(a, flip):
+    pairs = [(p * 2 + b, (7 - p) * 2 + (b ^ flip)) for b in range(2) for p in range(8)]
+    return lax.ppermute(a, ("pipe", "dp"), pairs)
+
+
+def swap_dp(a):
+    return lax.ppermute(a, "dp", [(0, 1), (1, 0)])
+
+
+def gather_items(pick, b):
+    return [
+        pick(0, b),
+        swap_dp(pick(0, 1 - b)),
+        mirror(pick(1, b), 0),
+        mirror(pick(1, 1 - b), 1),
+    ]
+
+
+def grad_kernel(sc, *refs):
+    xn_ctx, xn_oth, dy, dy_oth, dqkv = refs[0:4], refs[4], refs[5:9], refs[9], refs[10:14]
+    grad_qkv, grad_out = refs[14:]
+    step, wide = grad_out.shape
+    half = xn_oth.shape[1]
+    c = sc[2]
+    rows = pl.ds(pl.multiple_of(pl.program_id(0) * step, step), step)
+
+    def left(items, others):
+        return jnp.concatenate([r[:, rows] for r in items] + [others[:, rows]], axis=0)
+
+    def right(items, base, count, j):
+        starts = [base + side * count * wide + j * wide for side in (c, 1 - c)]
+        return jnp.concatenate(
+            [r[:, pl.ds(pl.multiple_of(start, 128), wide)] for start in starts for r in items],
+            axis=0,
+        )
+
+    lhs = left(xn_ctx, xn_oth)
+    for j in range(3):
+        grad_qkv[j] = dot_tn(lhs, right(dqkv, 0, 3, j)) * 0.5
+    grad_out[...] = dot_tn(left(dy, dy_oth), right(xn_ctx, half, 1, 0)) * 0.5
+
+
+def grad_call(sc, xn_ctx, xn_oth, dy, dy_oth, dqkv, wide):
+    half = xn_oth.shape[1]
+    step = 256
+    items = (*xn_ctx, xn_oth, *dy, dy_oth, *dqkv)
+    return pl.pallas_call(
+        grad_kernel,
+        grid=(half // step,),
+        out_shape=[
+            jax.ShapeDtypeStruct((3, half, wide), F32),
+            jax.ShapeDtypeStruct((half, wide), F32),
+        ],
+        in_specs=[SM] + [pl.BlockSpec(a.shape, lambda i: (0, 0)) for a in items],
+        out_specs=[
+            pl.BlockSpec((3, step, wide), lambda i: (0, i, 0)),
+            pl.BlockSpec((step, wide), lambda i: (i, 0)),
+        ],
+        compiler_params=pltpu.CompilerParams(vmem_limit_bytes=VMEM_LIMIT),
+        name="grad",
+    )(sc, *items)
 
 
 def doc_mask(doc_lengths, row_count):
@@ -325,7 +393,7 @@
                 axis=0,
             )
         )
-    return halves[0], halves[1], halves[0][48:]
+    return halves[0], halves[1], halves[0][:16]
 
 
 def mean(x):
@@ -347,6 +415,9 @@
     gain = jnp.concatenate([down_gain, up_gain], axis=0).astype(F32)
     allowed = jnp.stack([doc_mask(lengths[r, 0], rows) for r in range(2)]).astype(F32)
 
+    def after(value, *others):
+        return lax.optimization_barrier((value,) + others)[0]
+
     def scalars(is_down, is_up):
         active = (is_down | is_up).astype(jnp.int32)
         return jnp.stack([active, is_up.astype(jnp.int32), c, z]).astype(jnp.int32)
@@ -356,10 +427,10 @@
             ((2, rows, width), BF16),
             ((2, 3, rows, wide), BF16),
             ((2, 3, rows, rows), F32),
-            ((2, rows, wide), BF16),
+            ((2, rows // 2, 2 * wide), BF16),
         ]
     )
-    dy_state, dqkv_state = alloc([((2, rows, width), BF16), ((2, 3, rows, wide), BF16)])
+    dy_state, dqkv_state = alloc([((2, rows, width), BF16), ((2, rows // 2, 6 * wide), BF16)])
 
     own, oth, block = in_pieces(jnp.where(place == 0, inputs[0], inputs[1]), z, c)
     kept = [block, block]
@@ -375,11 +446,36 @@
         else:
             state = front_call(True, sc, own, oth, gain, allowed, weights, state)
     xn, qkv, prob, ctx = state
+    b = lax.axis_index("dp")
+
+    half = width // 2
+
+    def features(a, which, core):
+        return lax.dynamic_slice(a, (64 * core, which * half), (64, half))
+
+    def other_halves(local_whole, items):
+        received = other_core(jnp.concatenate([a[:, :half] for a in items[1:]], axis=0))
+        return jnp.concatenate([features(local_whole, b, 1 - c), received], axis=0)
+
+    xn_ctx = gather_items(
+        lambda d, which: jnp.concatenate([features(xn[d], which, c), ctx[d]], axis=1), b
+    )
+    xn_oth = other_halves(xn[0], xn_ctx)
 
     x = jnp.stack(kept).astype(F32)
     xc = x - mean(x)
     rstd = lax.rsqrt(mean(xc * xc) + EPS)
     xhat = xc * rstd
+
+    def tokens(own, oth):
+        first, second = jnp.where(c == 0, own, oth), jnp.where(c == 0, oth, own)
+        turned = jnp.concatenate([first, second], axis=0).reshape(2, 4, 16, width)
+        order = [lax.rem(z + 4 - k, 4) for k in SHIFTS]
+        blocks = [turned[:, 0]] * 4
+        for place_to in range(4):
+            for i in range(4):
+                blocks[place_to] = jnp.where(order[i] == place_to, turned[:, i], blocks[place_to])
+        return jnp.stack(blocks, axis=1).reshape(rows, width)
 
     own, oth, block = in_pieces(jnp.where(place == 7, cotangent[0], cotangent[1]), z, c)
     for t in range(8):
@@ -396,48 +492,24 @@
             change = rstd_d * (gr - mean(gr) - xhat_d * mean(gr * xhat_d))
             result = (block.astype(F32) + change).astype(BF16)
             own, oth, block = hop_and_spread(result, t)
+            if t == 1:
+                own, oth, block, xn_oth, *xn_ctx = lax.optimization_barrier(
+                    (own, oth, block, xn_oth, *xn_ctx)
+                )
         else:
+            dy_now = [
+                jnp.where(here, tokens(own, oth), dy_state[d])
+                for d, here in enumerate((is_down, is_up))
+            ]
+            dy = gather_items(lambda d, which: features(dy_now[d], which, c), b)
+            dy_oth = other_halves(dy_now[0], dy)
             dy_state, dqkv_state = back_call(
                 True, sc, own, oth, weights, qkv, prob, dy_state, dqkv_state
             )
 
-    b = lax.axis_index("dp")
-    half = width // 2
-
-    def feature_half(a, which):
-        return lax.dynamic_slice_in_dim(a, which * half, half, axis=-1)
-
-    def pack(d, which):
-        return jnp.concatenate(
-            [
-                feature_half(xn[d], which),
-                feature_half(dy_state[d], which),
-                ctx[d],
-                dqkv_state[d, 0],
-                dqkv_state[d, 1],
-                dqkv_state[d, 2],
-            ],
-            axis=1,
-        )
-
-    def mirror(a, flip):
-        pairs = [(p * 2 + bb, (7 - p) * 2 + (bb ^ flip)) for bb in range(2) for p in range(8)]
-        return lax.ppermute(a, ("pipe", "dp"), pairs)
-
-    packs = [
-        pack(0, b),
-        lax.ppermute(pack(0, 1 - b), "dp", [(0, 1), (1, 0)]),
-        mirror(pack(1, b), 0),
-        mirror(pack(1, 1 - b), 1),
-    ]
-    every = jnp.concatenate(packs, axis=0)
-    xn_all = every[:, :half]
-    dy_all = every[:, half : 2 * half]
-    ctx_all = every[:, 2 * half : 2 * half + wide]
-    dqkv_all = every[:, 2 * half + wide :]
-    grad_qkv = dot_tn(xn_all, dqkv_all) * 0.5
-    grad_out = dot_tn(dy_all, ctx_all) * 0.5
-    return grad_qkv.reshape(1, half, 3, wide), grad_out.reshape(1, half, wide)
+    dqkv = gather_items(lambda d, which: dqkv_state[d], b)
+    grad_qkv, grad_out = grad_call(sc, xn_ctx, xn_oth, dy, dy_oth, dqkv, wide)
+    return jnp.transpose(grad_qkv, (1, 0, 2))[None], grad_out[None]
 
 
 def solution(mesh):

time: 602 us -> 496 us (0.82)
  local copies, waits for them, and re-layouts: 83.9 us -> 5.44 us
  starting transfers between devices: 244 us -> 227 us
  matrix products: 7.77 us -> 0 us
  other arithmetic: 15.8 us -> 9.62 us
  Pallas kernels: 31.9 us -> 38 us
    unnamed x213 -> x67, local copies, waits for them, and re-layouts: 74.6 us -> 3.84 us
    ppermute x2 -> x6, waiting for transfers between devices: 62.9 us -> 18.1 us  [mirror(): return lax.ppermute(a, ('pipe', 'dp'), pairs)]
    ppermute x126 -> x128, waiting for transfers between devices: 148 us -> 178 us  [permute(): return lax.ppermute(x, AXES, pairs)]
    ppermute x126 -> x128, starting transfers between devices: 239 us -> 209 us  [permute(): return lax.ppermute(x, AXES, pairs)]
    ppermute x1 -> x3, waiting for transfers between devices: 0.01 us -> 8.37 us  [swap_dp(): return lax.ppermute(a, 'dp', [(0, 1), (1, 0)])]
    dot_general x2 -> x0, matrix products: 7.77 us -> none  [dot_tn(): lax.dot_general(a, b, (((0,), (0,)), ((), ())), preferred_element_type=F32)]
    pallas_call x0 -> x1, Pallas kernels: none -> 7.25 us  [grad_call(): pl.pallas_call(grad_kernel, grid=(half // step,), out_shape=[jax.ShapeDty...]
    ppermute x1 -> x3, starting transfers between devices: 0.51 us -> 7.06 us  [swap_dp(): return lax.ppermute(a, 'dp', [(0, 1), (1, 0)])]
  transfers between devices with their start and end apart: 129 -> 137, of which waited for: 89 -> 80; matrix products, arithmetic and copies ran while one was open for 2% -> 1% of each run, Pallas kernels for 0% -> 1%
where the time goes in v2:
time: 496 us; the launch traced here: 488 us
  starting transfers between devices  227 us (46%)
  waiting for transfers between devices  205 us (41%)
  Pallas kernels  38 us (8%)
  other arithmetic  9.62 us (2%)
  local copies, waits for them, and re-layouts  5.44 us (1%)
    ppermute x128, starting transfers between devices, permute(): return lax.ppermute(x, AXES, pairs)  209 us
    ppermute x128, waiting for transfers between devices, permute(): return lax.ppermute(x, AXES, pairs)  178 us
    ppermute x6, waiting for transfers between devices, mirror(): return lax.ppermute(a, ('pipe', 'dp'), pairs)  18.1 us
    pallas_call x8, Pallas kernels, front_call(): pl.pallas_call(functools.partial(front_kernel, last), out_shape=halves +...  15.9 us
    pallas_call x8, Pallas kernels, back_call(): pl.pallas_call(functools.partial(back_kernel, last), out_shape=halves + [...  14.9 us
    ppermute x6, starting transfers between devices, mirror(): return lax.ppermute(a, ('pipe', 'dp'), pairs)  10.8 us
  transfers between devices with their start and end apart: 137, of which 80 were waited for; matrix products, arithmetic and copies ran while one was open for 1% of the time, Pallas kernels for 1%

profile of v2, /device:TPU:1, one launch (start us, length us, event | category | flops | bytes accessed | tf_op | source)
XLA Modules:
  0.0 487.7 jit_solution(17882293684118583339)
XLA Ops:
  4.6 5.9 %front.8 = (bf16[64,2560]{1,0:T(8,128)(2,1)S(1)}, bf16[64,2560]{1,0:T(8,128)(2,1)S(1)}, bf16[2,128,2560]{2,1,0:T(8,128)(2,1)}, bf16[2,3,128,384]{3,2,1,0:T(8,128...) custom-call(s32[4]{0:T(128)S(1)} %add_add_fusion.sc, ...), custom_call_target="tpu_custom_call", output_to_operand_aliasing={{2}: (9, {}), {3}: (10, {}), {4}: (11, {}), {5}: (12, {})} | custom-call | flops 1006632960 | bytes 7864320 | tf_op jit(solution)/shard_map/front/pallas_call | solution.py:205
  27.9 5.3 %collective-permute-done.5 = bf16[16,2560]{1,0:T(8,128)(2,1)S(1)} collective-permute-done((bf16[16,2560]{1,0:T(8,128)(2,1)S(1)}, bf16[16,2560]{1,0:T(8,128)(2,1)S(1)}, u32[]{:S(2)}, u32[]{:S(2)}) %collective-permute-start.5) | collective-permute-done | bytes 81952 | tf_op jit(solution)/shard_map/ppermute | solution.py:289
  78.2 6.2 %collective-permute-done.23 = bf16[16,2560]{1,0:T(8,128)(2,1)S(1)} collective-permute-done((bf16[16,2560]{1,0:T(8,128)(2,1)S(1)}, bf16[16,2560]{1,0:T(8,128)(2,1)S(1)}, u32[]{:S(2)}, u32[]{:S(2)}) %collective-permute-start.23) | collective-permute-done | bytes 81952 | tf_op jit(solution)/shard_map/ppermute | solution.py:289
  101.0 5.6 %collective-permute-start.33 = (bf16[16,2560]{1,0:T(8,128)(2,1)S(1)}, bf16[16,2560]{1,0:T(8,128)(2,1)S(1)}, u32[]{:S(2)}, u32[]{:S(2)}) collective-permute-start(bf16[16,2560]{1,0:T(8,128)(2,1)S(1)} %add_convert_fusion.17), channel_id=1, source_target_pairs={{0,124},{2,126},{4,112},{6,114},{8,116},{10,118},{12,120},{14,122}... | collective-permute-start | bytes 245768 | tf_op jit(solution)/shard_map/ppermute | solution.py:289
  106.6 7.5 %collective-permute-done.32 = bf16[16,2560]{1,0:T(8,128)(2,1)S(1)} collective-permute-done((bf16[16,2560]{1,0:T(8,128)(2,1)S(1)}, bf16[16,2560]{1,0:T(8,128)(2,1)S(1)}, u32[]{:S(2)}, u32[]{:S(2)}) %collective-permute-start.32) | collective-permute-done | bytes 81952 | tf_op jit(solution)/shard_map/ppermute | solution.py:289
  132.1 4.8 collective-permute-done.41
  150.2 18.0 %collective-permute-start.49 = (bf16[16,2560]{1,0:T(8,128)(2,1)S(1)}, bf16[16,2560]{1,0:T(8,128)(2,1)S(1)}, u32[]{:S(2)}, u32[]{:S(2)}) collective-permute-start(bf16[16,2560]{1,0:T(8,128)(2,1)S(1)} %add_convert_fusion.15), channel_id=1, source_target_pairs={{0,48},{2,50},{4,52},{6,54},{8,56},{10,58},{12,60},{14,62},{16,32}... | collective-permute-start | bytes 245768 | tf_op jit(solution)/shard_map/ppermute | solution.py:289
  172.2 6.6 %collective-permute-done.50 = bf16[16,2560]{1,0:T(8,128)(2,1)S(1)} collective-permute-done((bf16[16,2560]{1,0:T(8,128)(2,1)S(1)}, bf16[16,2560]{1,0:T(8,128)(2,1)S(1)}, u32[]{:S(2)}, u32[]{:S(2)}) %collective-permute-start.50) | collective-permute-done | bytes 81952 | tf_op jit(solution)/shard_map/ppermute | solution.py:289
  192.7 8.6 %collective-permute-start.58 = (bf16[16,2560]{1,0:T(8,128)(2,1)S(1)}, bf16[16,2560]{1,0:T(8,128)(2,1)S(1)}, u32[]{:S(2)}, u32[]{:S(2)}) collective-permute-start(bf16[16,2560]{1,0:T(8,128)(2,1)S(1)} %add_convert_fusion.14), channel_id=1, source_target_pairs={{0,16},{2,18},{4,20},{6,22},{8,24},{10,26},{12,28},{14,30},{16,0},... | collective-permute-start | bytes 245768 | tf_op jit(solution)/shard_map/ppermute | solution.py:289
  205.2 5.7 %collective-permute-done.59 = bf16[16,2560]{1,0:T(8,128)(2,1)S(1)} collective-permute-done((bf16[16,2560]{1,0:T(8,128)(2,1)S(1)}, bf16[16,2560]{1,0:T(8,128)(2,1)S(1)}, u32[]{:S(2)}, u32[]{:S(2)}) %collective-permute-start.59) | collective-permute-done | bytes 81952 | tf_op jit(solution)/shard_map/ppermute | solution.py:289
  214.5 5.7 %front.15 = (bf16[2,128,2560]{2,1,0:T(8,128)(2,1)}, bf16[2,3,128,384]{3,2,1,0:T(8,128)(2,1)S(1)}, f32[2,3,128,128]{3,2,1,0:T(8,128)S(1)}, bf16[2,64,768]{2,1,0:T(8,128)(2,1)S(1)}) custom-call(s32[4]{0:T(128)S(1)} %add_add_fusion.7.sc, ...), custom_call_target="tpu_custom_call", output_to_operand_aliasing={{0}: (9, {}), {1}: (10, {}), {2}: (11, {}), {3}: (12, {})} | custom-call | flops 1006632960 | bytes 7864320 | tf_op jit(solution)/shard_map/front/pallas_call | solution.py:205
  221.0 7.1 %back.8 = (bf16[64,2560]{1,0:T(8,128)(2,1)S(1)}, bf16[64,2560]{1,0:T(8,128)(2,1)S(1)}, bf16[2,128,2560]{2,1,0:T(8,128)(2,1)}, bf16[2,64,2304]{2,1,0:T(8,128)(2,1)}) custom-call(s32[4]{0:T(128)S(1)} %add_add_fusion.7.sc, bf16[64,2560]{1,0:T(8,128)(2,1)S(1)} %get-tuple-element.313.own, ...), custom_call_target="tpu_custom_call", output_to_operand_aliasing={{2}: (9, {}), {3}: (10, {})} | custom-call | flops 1006632960 | bytes 7864320 | tf_op jit(solution)/shard_map/back/pallas_call | solution.py:234
  241.1 5.5 %collective-permute-done.68 = bf16[16,2560]{1,0:T(8,128)(2,1)S(1)} collective-permute-done((bf16[16,2560]{1,0:T(8,128)(2,1)S(1)}, bf16[16,2560]{1,0:T(8,128)(2,1)S(1)}, u32[]{:S(2)}, u32[]{:S(2)}) %collective-permute-start.68) | collective-permute-done | bytes 81952 | tf_op jit(solution)/shard_map/ppermute | solution.py:289
  276.9 6.6 %collective-permute-done.77 = bf16[16,2560]{1,0:T(8,128)(2,1)S(1)} collective-permute-done((bf16[16,2560]{1,0:T(8,128)(2,1)S(1)}, bf16[16,2560]{1,0:T(8,128)(2,1)S(1)}, u32[]{:S(2)}, u32[]{:S(2)}) %collective-permute-start.77) | collective-permute-done | bytes 81952 | tf_op jit(solution)/shard_map/ppermute | solution.py:289
  299.9 5.6 %collective-permute-done.90 = bf16[16,2560]{1,0:T(8,128)(2,1)S(1)} collective-permute-done((bf16[16,2560]{1,0:T(8,128)(2,1)S(1)}, bf16[16,2560]{1,0:T(8,128)(2,1)S(1)}, u32[]{:S(2)}, u32[]{:S(2)}) %collective-permute-start.90) | collective-permute-done | bytes 81952 | tf_op jit(solution)/shard_map/ppermute | solution.py:289
  327.4 5.9 %collective-permute-done.99 = bf16[16,2560]{1,0:T(8,128)(2,1)S(1)} collective-permute-done((bf16[16,2560]{1,0:T(8,128)(2,1)S(1)}, bf16[16,2560]{1,0:T(8,128)(2,1)S(1)}, u32[]{:S(2)}, u32[]{:S(2)}) %collective-permute-start.99) | collective-permute-done | bytes 81952 | tf_op jit(solution)/shard_map/ppermute | solution.py:289
  351.7 5.8 %collective-permute-done.108 = bf16[16,2560]{1,0:T(8,128)(2,1)S(1)} collective-permute-done((bf16[16,2560]{1,0:T(8,128)(2,1)S(1)}, bf16[16,2560]{1,0:T(8,128)(2,1)S(1)}, u32[]{:S(2)}, u32[]{:S(2)}) %collective-permute-start.108) | collective-permute-done | bytes 81952 | tf_op jit(solution)/shard_map/ppermute | solution.py:289
  370.5 18.4 %collective-permute-start.116 = (bf16[16,2560]{1,0:T(8,128)(2,1)S(1)}, bf16[16,2560]{1,0:T(8,128)(2,1)S(1)}, u32[]{:S(2)}, u32[]{:S(2)}) collective-permute-start(bf16[16,2560]{1,0:T(8,128)(2,1)S(1)} %fusion.12), channel_id=1, source_target_pairs={{0,48},{2,50},{4,52},{6,54},{8,56},{10,58},{12,60},{14,62},{16,32}... | collective-permute-start | bytes 245768 | tf_op jit(solution)/shard_map/ppermute | solution.py:289
  393.6 6.6 %collective-permute-done.117 = bf16[16,2560]{1,0:T(8,128)(2,1)S(1)} collective-permute-done((bf16[16,2560]{1,0:T(8,128)(2,1)S(1)}, bf16[16,2560]{1,0:T(8,128)(2,1)S(1)}, u32[]{:S(2)}, u32[]{:S(2)}) %collective-permute-start.117) | collective-permute-done | bytes 81952 | tf_op jit(solution)/shard_map/ppermute | solution.py:289
  414.3 10.2 %collective-permute-start.125 = (bf16[16,2560]{1,0:T(8,128)(2,1)S(1)}, bf16[16,2560]{1,0:T(8,128)(2,1)S(1)}, u32[]{:S(2)}, u32[]{:S(2)}) collective-permute-start(bf16[16,2560]{1,0:T(8,128)(2,1)S(1)} %fusion.7), channel_id=1, source_target_pairs={{0,16},{2,18},{4,20},{6,22},{8,24},{10,26},{12,28},{14,30},{16,0},... | collective-permute-start | bytes 245768 | tf_op jit(solution)/shard_map/ppermute | solution.py:289
  428.2 5.8 %collective-permute-done.126 = bf16[16,2560]{1,0:T(8,128)(2,1)S(1)} collective-permute-done((bf16[16,2560]{1,0:T(8,128)(2,1)S(1)}, bf16[16,2560]{1,0:T(8,128)(2,1)S(1)}, u32[]{:S(2)}, u32[]{:S(2)}) %collective-permute-start.126) | collective-permute-done | bytes 81952 | tf_op jit(solution)/shard_map/ppermute | solution.py:289
  461.9 8.1 %collective-permute-done.136.refs_13_ = bf16[64,2304]{1,0:T(8,128)(2,1)S(1)} collective-permute-done((bf16[64,2304]{1,0:T(8,128)(2,1)S(1)}, bf16[64,2304]{1,0:T(8,128)(2,1)S(1)}, u32[]{:S(2)}, u32[]{:S(2)}) %collective-permute-start.136) | collective-permute-done | bytes 294944 | tf_op jit(solution)/shard_map/ppermute | solution.py:316
  472.9 6.4 %collective-permute-done.134.refs_11_ = bf16[64,2304]{1,0:T(8,128)(2,1)S(1)} collective-permute-done((bf16[64,2304]{1,0:T(8,128)(2,1)S(1)}, bf16[64,2304]{1,0:T(8,128)(2,1)S(1)}, u32[]{:S(2)}, u32[]{:S(2)}) %collective-permute-start.134) | collective-permute-done | bytes 294944 | tf_op jit(solution)/shard_map/ppermute | solution.py:320
  480.1 7.3 %grad.1 = (f32[3,1280,384]{2,1,0:T(8,128)}, f32[1280,384]{1,0:T(8,128)}) custom-call(s32[4]{0:T(128)S(1)} %add_add_fusion.sc, bf16[64,2048]{1,0:T(8,128)(2,1)S(1)} %get-tuple-element.151.refs_0_, bf16[64,2048]{1,0:T(8,128)(2,1)S(1)} %collective-permute-done.81.refs_1_, bf16[64,2048]{1,0:T(8,128)(2,1)S(1)} %collective-permute-done.82.refs_2_, ...), custom_call_target="tpu_custom_call" | custom-call | tf_op jit(solution)/shard_map/grad/pallas_call | solution.py:360
  (466 shorter events, 305.8 us)
Async XLA Ops:
  22.3 11.0 %collective-permute-start.7 = (bf16[16,2560]{1,0:T(8,128)(2,1)S(1)}, bf16[16,2560]{1,0:T(8,128)(2,1)S(1)}, u32[]{:S(2)}, u32[]{:S(2)}) collective-permute-start(bf16[16,2560]{1,0:T(8,128)(2,1)S(1)} %add_convert_fusion.20), channel_id=1, source_target_pairs={{0,24},{2,26},{4,28},{6,30},{8,16},{10,18},{12,20},{14,22},{16,8},... | collective-permute-start | bytes 245768 | tf_op jit(solution)/shard_map/ppermute | solution.py:289
  45.7 12.0 %collective-permute-start.16 = (bf16[16,2560]{1,0:T(8,128)(2,1)S(1)}, bf16[16,2560]{1,0:T(8,128)(2,1)S(1)}, u32[]{:S(2)}, u32[]{:S(2)}) collective-permute-start(bf16[16,2560]{1,0:T(8,128)(2,1)S(1)} %add_convert_fusion.19), channel_id=1, source_target_pairs={{0,56},{2,58},{4,60},{6,62},{8,48},{10,50},{12,52},{14,54},{16,40}... | collective-permute-start | bytes 245768 | tf_op jit(solution)/shard_map/ppermute | solution.py:289
  100.9 13.3 %collective-permute-start.34 = (bf16[16,2560]{1,0:T(8,128)(2,1)S(1)}, bf16[16,2560]{1,0:T(8,128)(2,1)S(1)}, u32[]{:S(2)}, u32[]{:S(2)}) collective-permute-start(bf16[16,2560]{1,0:T(8,128)(2,1)S(1)} %add_convert_fusion.17), channel_id=1, source_target_pairs={{0,120},{2,122},{4,124},{6,126},{8,112},{10,114},{12,116},{14,118}... | collective-permute-start | bytes 245768 | tf_op jit(solution)/shard_map/ppermute | solution.py:289
  101.0 13.1 %collective-permute-start.33 = (bf16[16,2560]{1,0:T(8,128)(2,1)S(1)}, bf16[16,2560]{1,0:T(8,128)(2,1)S(1)}, u32[]{:S(2)}, u32[]{:S(2)}) collective-permute-start(bf16[16,2560]{1,0:T(8,128)(2,1)S(1)} %add_convert_fusion.17), channel_id=1, source_target_pairs={{0,124},{2,126},{4,112},{6,114},{8,116},{10,118},{12,120},{14,122}... | collective-permute-start | bytes 245768 | tf_op jit(solution)/shard_map/ppermute | solution.py:289
  150.2 22.1 %collective-permute-start.49 = (bf16[16,2560]{1,0:T(8,128)(2,1)S(1)}, bf16[16,2560]{1,0:T(8,128)(2,1)S(1)}, u32[]{:S(2)}, u32[]{:S(2)}) collective-permute-start(bf16[16,2560]{1,0:T(8,128)(2,1)S(1)} %add_convert_fusion.15), channel_id=1, source_target_pairs={{0,48},{2,50},{4,52},{6,54},{8,56},{10,58},{12,60},{14,62},{16,32}... | collective-permute-start | bytes 245768 | tf_op jit(solution)/shard_map/ppermute | solution.py:289
  168.2 10.7 %collective-permute-start.52 = (bf16[16,2560]{1,0:T(8,128)(2,1)S(1)}, bf16[16,2560]{1,0:T(8,128)(2,1)S(1)}, u32[]{:S(2)}, u32[]{:S(2)}) collective-permute-start(bf16[16,2560]{1,0:T(8,128)(2,1)S(1)} %add_convert_fusion.15), channel_id=1, source_target_pairs={{0,56},{2,58},{4,60},{6,62},{8,48},{10,50},{12,52},{14,54},{16,40}... | collective-permute-start | bytes 245768 | tf_op jit(solution)/shard_map/ppermute | solution.py:289
  168.7 10.2 %collective-permute-start.51 = (bf16[16,2560]{1,0:T(8,128)(2,1)S(1)}, bf16[16,2560]{1,0:T(8,128)(2,1)S(1)}, u32[]{:S(2)}, u32[]{:S(2)}) collective-permute-start(bf16[16,2560]{1,0:T(8,128)(2,1)S(1)} %add_convert_fusion.15), channel_id=1, source_target_pairs={{0,60},{2,62},{4,48},{6,50},{8,52},{10,54},{12,56},{14,58},{16,44}... | collective-permute-start | bytes 245768 | tf_op jit(solution)/shard_map/ppermute | solution.py:289
  192.7 12.4 %collective-permute-start.58 = (bf16[16,2560]{1,0:T(8,128)(2,1)S(1)}, bf16[16,2560]{1,0:T(8,128)(2,1)S(1)}, u32[]{:S(2)}, u32[]{:S(2)}) collective-permute-start(bf16[16,2560]{1,0:T(8,128)(2,1)S(1)} %add_convert_fusion.14), channel_id=1, source_target_pairs={{0,16},{2,18},{4,20},{6,22},{8,24},{10,26},{12,28},{14,30},{16,0},... | collective-permute-start | bytes 245768 | tf_op jit(solution)/shard_map/ppermute | solution.py:289
  249.1 14.6 %collective-permute-start.82 = (bf16[64,2048]{1,0:T(8,128)(2,1)S(1)}, bf16[64,2048]{1,0:T(8,128)(2,1)S(1)}, u32[]{:S(2)}, u32[]{:S(2)}) collective-permute-start(bf16[64,2048]{1,0:T(8,128)(2,1)S(1)} %get-tuple-element.297), channel_id=1, source_target_pairs={{0,112},{16,96},{32,80},{48,64},{64,48},{80,32},{96,16},{112,0},{1... | collective-permute-start | bytes 786440 | tf_op jit(solution)/shard_map/ppermute | solution.py:316
  249.8 14.1 %collective-permute-start.83 = (bf16[64,2048]{1,0:T(8,128)(2,1)S(1)}, bf16[64,2048]{1,0:T(8,128)(2,1)S(1)}, u32[]{:S(2)}, u32[]{:S(2)}) collective-permute-start(bf16[64,2048]{1,0:T(8,128)(2,1)S(1)} %get-tuple-element.298), channel_id=1, source_target_pairs={{0,113},{16,97},{32,81},{48,65},{64,49},{80,33},{96,17},{112,1},{1... | collective-permute-start | bytes 786440 | tf_op jit(solution)/shard_map/ppermute | solution.py:316
  268.6 16.3 %collective-permute-start.84 = (bf16[192,1280]{1,0:T(8,128)(2,1)S(1)}, bf16[192,1280]{1,0:T(8,128)(2,1)S(1)}, u32[]{:S(2)}, u32[]{:S(2)}) collective-permute-start(bf16[192,1280]{1,0:T(8,128)(2,1)S(1)} %pad_maximum_fusion.4), channel_id=1, source_target_pairs={{0,2},{2,0},{4,6},{6,4},{8,10},{10,8},{12,14},{14,12},{16,18},{18,... | collective-permute-start | bytes 1474568 | tf_op jit(solution)/shard_map/ppermute | solution.py:289
  271.6 12.0 %collective-permute-start.79 = (bf16[16,2560]{1,0:T(8,128)(2,1)S(1)}, bf16[16,2560]{1,0:T(8,128)(2,1)S(1)}, u32[]{:S(2)}, u32[]{:S(2)}) collective-permute-start(bf16[16,2560]{1,0:T(8,128)(2,1)S(1)} %fusion.32), channel_id=1, source_target_pairs={{0,56},{2,58},{4,60},{6,62},{8,48},{10,50},{12,52},{14,54},{16,40}... | collective-permute-start | bytes 245768 | tf_op jit(solution)/shard_map/ppermute | solution.py:289
  320.1 13.3 %collective-permute-start.101 = (bf16[16,2560]{1,0:T(8,128)(2,1)S(1)}, bf16[16,2560]{1,0:T(8,128)(2,1)S(1)}, u32[]{:S(2)}, u32[]{:S(2)}) collective-permute-start(bf16[16,2560]{1,0:T(8,128)(2,1)S(1)} %fusion.22), channel_id=1, source_target_pairs={{0,120},{2,122},{4,124},{6,126},{8,112},{10,114},{12,116},{14,118}... | collective-permute-start | bytes 245768 | tf_op jit(solution)/shard_map/ppermute | solution.py:289
  322.9 10.4 %collective-permute-start.100 = (bf16[16,2560]{1,0:T(8,128)(2,1)S(1)}, bf16[16,2560]{1,0:T(8,128)(2,1)S(1)}, u32[]{:S(2)}, u32[]{:S(2)}) collective-permute-start(bf16[16,2560]{1,0:T(8,128)(2,1)S(1)} %fusion.22), channel_id=1, source_target_pairs={{0,124},{2,126},{4,112},{6,114},{8,116},{10,118},{12,120},{14,122}... | collective-permute-start | bytes 245768 | tf_op jit(solution)/shard_map/ppermute | solution.py:289
  370.5 23.1 %collective-permute-start.116 = (bf16[16,2560]{1,0:T(8,128)(2,1)S(1)}, bf16[16,2560]{1,0:T(8,128)(2,1)S(1)}, u32[]{:S(2)}, u32[]{:S(2)}) collective-permute-start(bf16[16,2560]{1,0:T(8,128)(2,1)S(1)} %fusion.12), channel_id=1, source_target_pairs={{0,48},{2,50},{4,52},{6,54},{8,56},{10,58},{12,60},{14,62},{16,32}... | collective-permute-start | bytes 245768 | tf_op jit(solution)/shard_map/ppermute | solution.py:289
  388.9 11.3 %collective-permute-start.119 = (bf16[16,2560]{1,0:T(8,128)(2,1)S(1)}, bf16[16,2560]{1,0:T(8,128)(2,1)S(1)}, u32[]{:S(2)}, u32[]{:S(2)}) collective-permute-start(bf16[16,2560]{1,0:T(8,128)(2,1)S(1)} %fusion.12), channel_id=1, source_target_pairs={{0,56},{2,58},{4,60},{6,62},{8,48},{10,50},{12,52},{14,54},{16,40}... | collective-permute-start | bytes 245768 | tf_op jit(solution)/shard_map/ppermute | solution.py:289
  389.4 10.8 %collective-permute-start.118 = (bf16[16,2560]{1,0:T(8,128)(2,1)S(1)}, bf16[16,2560]{1,0:T(8,128)(2,1)S(1)}, u32[]{:S(2)}, u32[]{:S(2)}) collective-permute-start(bf16[16,2560]{1,0:T(8,128)(2,1)S(1)} %fusion.12), channel_id=1, source_target_pairs={{0,60},{2,62},{4,48},{6,50},{8,52},{10,54},{12,56},{14,58},{16,44}... | collective-permute-start | bytes 245768 | tf_op jit(solution)/shard_map/ppermute | solution.py:289
  414.3 13.9 %collective-permute-start.125 = (bf16[16,2560]{1,0:T(8,128)(2,1)S(1)}, bf16[16,2560]{1,0:T(8,128)(2,1)S(1)}, u32[]{:S(2)}, u32[]{:S(2)}) collective-permute-start(bf16[16,2560]{1,0:T(8,128)(2,1)S(1)} %fusion.7), channel_id=1, source_target_pairs={{0,16},{2,18},{4,20},{6,22},{8,24},{10,26},{12,28},{14,30},{16,0},... | collective-permute-start | bytes 245768 | tf_op jit(solution)/shard_map/ppermute | solution.py:289
  439.3 13.0 %collective-permute-start.132 = (bf16[64,1280]{1,0:T(8,128)(2,1)S(1)}, bf16[64,1280]{1,0:T(8,128)(2,1)S(1)}, u32[]{:S(2)}, u32[]{:S(2)}) collective-permute-start(bf16[64,1280]{1,0:T(8,128)(2,1)S(1)} %get-tuple-element.218), channel_id=1, source_target_pairs={{0,113},{16,97},{32,81},{48,65},{64,49},{80,33},{96,17},{112,1},{1... | collective-permute-start | bytes 491528 | tf_op jit(solution)/shard_map/ppermute | solution.py:316
  441.9 10.4 %collective-permute-start.131 = (bf16[64,1280]{1,0:T(8,128)(2,1)S(1)}, bf16[64,1280]{1,0:T(8,128)(2,1)S(1)}, u32[]{:S(2)}, u32[]{:S(2)}) collective-permute-start(bf16[64,1280]{1,0:T(8,128)(2,1)S(1)} %get-tuple-element.219), channel_id=1, source_target_pairs={{0,112},{16,96},{32,80},{48,64},{64,48},{80,32},{96,16},{112,0},{1... | collective-permute-start | bytes 491528 | tf_op jit(solution)/shard_map/ppermute | solution.py:316
  442.6 10.7 %collective-permute-start.130 = (bf16[64,1280]{1,0:T(8,128)(2,1)S(1)}, bf16[64,1280]{1,0:T(8,128)(2,1)S(1)}, u32[]{:S(2)}, u32[]{:S(2)}) collective-permute-start(bf16[64,1280]{1,0:T(8,128)(2,1)S(1)} %get-tuple-element.216), channel_id=1, source_target_pairs={{0,1},{1,0},{2,3},{3,2},{4,5},{5,4},{6,7},{7,6},{8,9},{9,8},{10,11... | collective-permute-start | bytes 491528 | tf_op jit(solution)/shard_map/ppermute | solution.py:320
  455.0 15.1 %collective-permute-start.136 = (bf16[64,2304]{1,0:T(8,128)(2,1)S(1)}, bf16[64,2304]{1,0:T(8,128)(2,1)S(1)}, u32[]{:S(2)}, u32[]{:S(2)}) collective-permute-start(bf16[64,2304]{1,0:T(8,128)(2,1)S(1)} %get-tuple-element.249), channel_id=1, source_target_pairs={{0,113},{16,97},{32,81},{48,65},{64,49},{80,33},{96,17},{112,1},{1... | collective-permute-start | bytes 884744 | tf_op jit(solution)/shard_map/ppermute | solution.py:316
  457.5 15.4 %collective-permute-start.135 = (bf16[64,2304]{1,0:T(8,128)(2,1)S(1)}, bf16[64,2304]{1,0:T(8,128)(2,1)S(1)}, u32[]{:S(2)}, u32[]{:S(2)}) collective-permute-start(bf16[64,2304]{1,0:T(8,128)(2,1)S(1)} %get-tuple-element.249), channel_id=1, source_target_pairs={{0,112},{16,96},{32,80},{48,64},{64,48},{80,32},{96,16},{112,0},{1... | collective-permute-start | bytes 884744 | tf_op jit(solution)/shard_map/ppermute | solution.py:316
  457.5 21.8 %collective-permute-start.134 = (bf16[64,2304]{1,0:T(8,128)(2,1)S(1)}, bf16[64,2304]{1,0:T(8,128)(2,1)S(1)}, u32[]{:S(2)}, u32[]{:S(2)}) collective-permute-start(bf16[64,2304]{1,0:T(8,128)(2,1)S(1)} %get-tuple-element.250.refs_10_), channel_id=1, source_target_pairs={{0,1},{1,0},{2,3},{3,2},{4,5},{5,4},{6,7},{7,6},{8,9},{9,8},{10,11... | collective-permute-start | bytes 884744 | tf_op jit(solution)/shard_map/ppermute | solution.py:320
  (126 other events, 721.8 us)

commit v3 on v2

--- a/solution.py
+++ b/solution.py
@@ -13,7 +13,7 @@
 BF16 = jnp.bfloat16
 SHIFTS = (0, 1, 3, 2)
 WEIGHT_PARTS = 2
-VMEM_LIMIT = 52 * 1024 * 1024
+VMEM_LIMIT = 24 * 1024 * 1024
 
 
 def dot_nn(a, b):
@@ -113,9 +113,9 @@
 
 def back_kernel(last, sc, own, oth, wd, wu, od, ou, qkv_i, prob_i, dy_i, dqkv_i, *refs):
     if last:
-        dy_o, dqkv_o, w, o, dy, qkv, prob, dqkv, wsem, ssem = refs
+        dy_o, dqkv_o, w, o, dy, qkv, prob, dqkv, grads, wsem, ssem = refs
     else:
-        keep, send, dy_o, dqkv_o, w, o, dy, qkv, prob, dqkv, wsem, ssem = refs
+        keep, send, dy_o, dqkv_o, w, o, dy, qkv, prob, dqkv, grads, wsem, ssem = refs
     active, d, c, z = sc[0], sc[1], sc[2], sc[3]
 
     @pl.when(active == 1)
@@ -146,15 +146,13 @@
             dp = dot_nt(dctx_h, qkv[2, :, cols])
             inner = jnp.sum(p * dp, axis=-1, keepdims=True)
             ds = (p * (dp - inner) * FACTOR).astype(BF16)
-            grads = (
-                dot_nn(ds, qkv[1, :, cols]).astype(BF16),
-                dot_tn(ds, qkv[0, :, cols]).astype(BF16),
-                dot_tn(p.astype(BF16), dctx_h).astype(BF16),
-            )
-            for j in range(3):
-                for side in range(2):
-                    at = (side * 3 + j) * 3 * HS + h * HS
-                    dqkv[:, at : at + HS] = grads[j][64 * side : 64 * side + 64]
+            grads[0, :, cols] = dot_nn(ds, qkv[1, :, cols]).astype(BF16)
+            grads[1, :, cols] = dot_tn(ds, qkv[0, :, cols]).astype(BF16)
+            grads[2, :, cols] = dot_tn(p.astype(BF16), dctx_h).astype(BF16)
+        for j in range(3):
+            for side in range(2):
+                at = (side * 3 + j) * 3 * HS
+                dqkv[:, at : at + 3 * HS] = grads[j, 64 * side : 64 * side + 64, :]
         copies.append(pltpu.make_async_copy(dqkv, dqkv_o.at[d], ssem.at[3]))
         copies[1].start()
         if not last:
@@ -163,7 +161,7 @@
                 lhs.append(
                     jnp.concatenate(
                         [
-                            dqkv[:, pl.ds(pl.multiple_of((side * 3 + j) * 3 * HS, HS), 3 * HS)]
+                            grads[j, pl.ds(pl.multiple_of(64 * side, 64), 64), :]
                             for side in (1 - c, c)
                         ],
                         axis=0,
@@ -189,7 +187,11 @@
 
 
 def like(a):
-    return jax.ShapeDtypeStruct(a.shape, a.dtype)
+    return pltpu.HBM(a.shape, a.dtype)
+
+
+def in_hbm(arrays):
+    return [pltpu.with_memory_space_constraint(a, pltpu.HBM) for a in arrays]
 
 
 def spread_like(rows, width):
@@ -223,7 +225,7 @@
             flops=2 * 128 * width * wide * 4, bytes_accessed=8 * width * wide, transcendentals=0
         ),
         name="front",
-    )(sc, own, oth, gain, allowed, *weights, *state)
+    )(sc, own, oth, gain, allowed, *in_hbm((*weights, *state)))
 
 
 def back_call(last, sc, own, oth, weights, qkv, prob, dy, dqkv):
@@ -244,6 +246,7 @@
             pltpu.VMEM(qkv.shape[1:], BF16),
             pltpu.VMEM(prob.shape[1:], F32),
             pltpu.VMEM(dqkv.shape[1:], BF16),
+            pltpu.VMEM(qkv.shape[1:], BF16),
             pltpu.SemaphoreType.DMA((4,)),
             pltpu.SemaphoreType.DMA((4,)),
         ],
@@ -252,7 +255,7 @@
             flops=2 * 128 * width * wide * 4, bytes_accessed=8 * width * wide, transcendentals=0
         ),
         name="back",
-    )(sc, own, oth, *weights, qkv, prob, dy, dqkv)
+    )(sc, own, oth, *in_hbm((*weights, qkv, prob, dy, dqkv)))
 
 
 def alloc_kernel(*refs):
@@ -262,7 +265,7 @@
 def alloc(shapes):
     return pl.pallas_call(
         alloc_kernel,
-        out_shape=[jax.ShapeDtypeStruct(s, t) for s, t in shapes],
+        out_shape=[pltpu.HBM(s, t) for s, t in shapes],
         out_specs=[ANY] * len(shapes),
         name="alloc",
     )()

time: 496 us -> 491 us (0.990)
  transfers between devices with their start and end apart: 137 -> 137, of which waited for: 80 -> 81; matrix products, arithmetic and copies ran while one was open for 1% -> 0% of each run, Pallas kernels for 1% -> 1%
where the time goes in v3:
time: 491 us; the launch traced here: 482 us
  starting transfers between devices  227 us (46%)
  waiting for transfers between devices  204 us (42%)
  Pallas kernels  37.4 us (8%)
  other arithmetic  7.85 us (2%)
    ppermute x128, starting transfers between devices, permute(): return lax.ppermute(x, AXES, pairs)  210 us
    ppermute x128, waiting for transfers between devices, permute(): return lax.ppermute(x, AXES, pairs)  178 us
    ppermute x6, waiting for transfers between devices, mirror(): return lax.ppermute(a, ('pipe', 'dp'), pairs)  18.5 us
    pallas_call x8, Pallas kernels, front_call(): pl.pallas_call(functools.partial(front_kernel, last), out_shape=halves +...  15.9 us
    pallas_call x8, Pallas kernels, back_call(): pl.pallas_call(functools.partial(back_kernel, last), out_shape=halves + [...  15.3 us
    ppermute x6, starting transfers between devices, mirror(): return lax.ppermute(a, ('pipe', 'dp'), pairs)  10.9 us
  transfers between devices with their start and end apart: 137, of which 81 were waited for; matrix products, arithmetic and copies ran while one was open for 0% of the time, Pallas kernels for 1%

profile of v3, /device:TPU:1, one launch (start us, length us, event | category | flops | bytes accessed | tf_op | source)
XLA Modules:
  0.0 482.3 jit_solution(9164810237910856514)
XLA Ops:
  3.8 5.8 %front.8 = (bf16[64,2560]{1,0:T(8,128)(2,1)S(1)}, bf16[64,2560]{1,0:T(8,128)(2,1)S(1)}, bf16[2,128,2560]{2,1,0:T(8,128)(2,1)}, bf16[2,3,128,384]{3,2,1,0:T(8,128...) custom-call(s32[4]{0:T(128)S(1)} %add_add_fusion.sc, ...), custom_call_target="tpu_custom_call", output_to_operand_aliasing={{2}: (9, {}), {3}: (10, {}), {4}: (11, {}), {5}: (12, {})} | custom-call | flops 1006632960 | bytes 7864320 | tf_op jit(solution)/shard_map/front/pallas_call | solution.py:207
  27.0 5.3 %collective-permute-done.5 = bf16[16,2560]{1,0:T(8,128)(2,1)S(1)} collective-permute-done((bf16[16,2560]{1,0:T(8,128)(2,1)S(1)}, bf16[16,2560]{1,0:T(8,128)(2,1)S(1)}, u32[]{:S(2)}, u32[]{:S(2)}) %collective-permute-start.5) | collective-permute-done | bytes 81952 | tf_op jit(solution)/shard_map/ppermute | solution.py:292
  77.2 6.2 %collective-permute-done.23 = bf16[16,2560]{1,0:T(8,128)(2,1)S(1)} collective-permute-done((bf16[16,2560]{1,0:T(8,128)(2,1)S(1)}, bf16[16,2560]{1,0:T(8,128)(2,1)S(1)}, u32[]{:S(2)}, u32[]{:S(2)}) %collective-permute-start.23) | collective-permute-done | bytes 81952 | tf_op jit(solution)/shard_map/ppermute | solution.py:292
  100.0 5.6 %collective-permute-start.33 = (bf16[16,2560]{1,0:T(8,128)(2,1)S(1)}, bf16[16,2560]{1,0:T(8,128)(2,1)S(1)}, u32[]{:S(2)}, u32[]{:S(2)}) collective-permute-start(bf16[16,2560]{1,0:T(8,128)(2,1)S(1)} %add_convert_fusion.17), channel_id=1, source_target_pairs={{0,124},{2,126},{4,112},{6,114},{8,116},{10,118},{12,120},{14,122}... | collective-permute-start | bytes 245768 | tf_op jit(solution)/shard_map/ppermute | solution.py:292
  105.6 7.5 %collective-permute-done.32 = bf16[16,2560]{1,0:T(8,128)(2,1)S(1)} collective-permute-done((bf16[16,2560]{1,0:T(8,128)(2,1)S(1)}, bf16[16,2560]{1,0:T(8,128)(2,1)S(1)}, u32[]{:S(2)}, u32[]{:S(2)}) %collective-permute-start.32) | collective-permute-done | bytes 81952 | tf_op jit(solution)/shard_map/ppermute | solution.py:292
  131.1 4.8 %collective-permute-done.41 = bf16[16,2560]{1,0:T(8,128)(2,1)S(1)} collective-permute-done((bf16[16,2560]{1,0:T(8,128)(2,1)S(1)}, bf16[16,2560]{1,0:T(8,128)(2,1)S(1)}, u32[]{:S(2)}, u32[]{:S(2)}) %collective-permute-start.41) | collective-permute-done | bytes 81952 | tf_op jit(solution)/shard_map/ppermute | solution.py:292
  149.1 17.6 %collective-permute-start.49 = (bf16[16,2560]{1,0:T(8,128)(2,1)S(1)}, bf16[16,2560]{1,0:T(8,128)(2,1)S(1)}, u32[]{:S(2)}, u32[]{:S(2)}) collective-permute-start(bf16[16,2560]{1,0:T(8,128)(2,1)S(1)} %add_convert_fusion.15), channel_id=1, source_target_pairs={{0,48},{2,50},{4,52},{6,54},{8,56},{10,58},{12,60},{14,62},{16,32}... | collective-permute-start | bytes 245768 | tf_op jit(solution)/shard_map/ppermute | solution.py:292
  170.8 6.6 %collective-permute-done.50 = bf16[16,2560]{1,0:T(8,128)(2,1)S(1)} collective-permute-done((bf16[16,2560]{1,0:T(8,128)(2,1)S(1)}, bf16[16,2560]{1,0:T(8,128)(2,1)S(1)}, u32[]{:S(2)}, u32[]{:S(2)}) %collective-permute-start.50) | collective-permute-done | bytes 81952 | tf_op jit(solution)/shard_map/ppermute | solution.py:292
  191.3 8.3 %collective-permute-start.58 = (bf16[16,2560]{1,0:T(8,128)(2,1)S(1)}, bf16[16,2560]{1,0:T(8,128)(2,1)S(1)}, u32[]{:S(2)}, u32[]{:S(2)}) collective-permute-start(bf16[16,2560]{1,0:T(8,128)(2,1)S(1)} %add_convert_fusion.14), channel_id=1, source_target_pairs={{0,16},{2,18},{4,20},{6,22},{8,24},{10,26},{12,28},{14,30},{16,0},... | collective-permute-start | bytes 245768 | tf_op jit(solution)/shard_map/ppermute | solution.py:292
  203.6 5.7 %collective-permute-done.59 = bf16[16,2560]{1,0:T(8,128)(2,1)S(1)} collective-permute-done((bf16[16,2560]{1,0:T(8,128)(2,1)S(1)}, bf16[16,2560]{1,0:T(8,128)(2,1)S(1)}, u32[]{:S(2)}, u32[]{:S(2)}) %collective-permute-start.59) | collective-permute-done | bytes 81952 | tf_op jit(solution)/shard_map/ppermute | solution.py:292
  212.8 5.7 %front.15 = (bf16[2,128,2560]{2,1,0:T(8,128)(2,1)}, bf16[2,3,128,384]{3,2,1,0:T(8,128)(2,1)}, f32[2,3,128,128]{3,2,1,0:T(8,128)}, bf16[2,64,768]{2,1,0:T(8,128)(2,1)}) custom-call(s32[4]{0:T(128)S(1)} %add_add_fusion.7.sc, ...), custom_call_target="tpu_custom_call", output_to_operand_aliasing={{0}: (9, {}), {1}: (10, {}), {2}: (11, {}), {3}: (12, {})} | custom-call | flops 1006632960 | bytes 7864320 | tf_op jit(solution)/shard_map/front/pallas_call | solution.py:207
  218.5 6.9 %back.8 = (bf16[64,2560]{1,0:T(8,128)(2,1)S(1)}, bf16[64,2560]{1,0:T(8,128)(2,1)S(1)}, bf16[2,128,2560]{2,1,0:T(8,128)(2,1)}, bf16[2,64,2304]{2,1,0:T(8,128)(2,1)}) custom-call(s32[4]{0:T(128)S(1)} %add_add_fusion.7.sc, bf16[64,2560]{1,0:T(8,128)(2,1)S(1)} %get-tuple-element.313.own, ...), custom_call_target="tpu_custom_call", output_to_operand_aliasing={{2}: (9, {}), {3}: (10, {})} | custom-call | flops 1006632960 | bytes 7864320 | tf_op jit(solution)/shard_map/back/pallas_call | solution.py:236
  238.4 5.5 %collective-permute-done.68 = bf16[16,2560]{1,0:T(8,128)(2,1)S(1)} collective-permute-done((bf16[16,2560]{1,0:T(8,128)(2,1)S(1)}, bf16[16,2560]{1,0:T(8,128)(2,1)S(1)}, u32[]{:S(2)}, u32[]{:S(2)}) %collective-permute-start.68) | collective-permute-done | bytes 81952 | tf_op jit(solution)/shard_map/ppermute | solution.py:292
  273.9 6.6 %collective-permute-done.77 = bf16[16,2560]{1,0:T(8,128)(2,1)S(1)} collective-permute-done((bf16[16,2560]{1,0:T(8,128)(2,1)S(1)}, bf16[16,2560]{1,0:T(8,128)(2,1)S(1)}, u32[]{:S(2)}, u32[]{:S(2)}) %collective-permute-start.77) | collective-permute-done | bytes 81952 | tf_op jit(solution)/shard_map/ppermute | solution.py:292
  296.8 5.6 %collective-permute-done.90 = bf16[16,2560]{1,0:T(8,128)(2,1)S(1)} collective-permute-done((bf16[16,2560]{1,0:T(8,128)(2,1)S(1)}, bf16[16,2560]{1,0:T(8,128)(2,1)S(1)}, u32[]{:S(2)}, u32[]{:S(2)}) %collective-permute-start.90) | collective-permute-done | bytes 81952 | tf_op jit(solution)/shard_map/ppermute | solution.py:292
  324.4 6.2 %collective-permute-done.99 = bf16[16,2560]{1,0:T(8,128)(2,1)S(1)} collective-permute-done((bf16[16,2560]{1,0:T(8,128)(2,1)S(1)}, bf16[16,2560]{1,0:T(8,128)(2,1)S(1)}, u32[]{:S(2)}, u32[]{:S(2)}) %collective-permute-start.99) | collective-permute-done | bytes 81952 | tf_op jit(solution)/shard_map/ppermute | solution.py:292
  348.7 5.8 %collective-permute-done.108 = bf16[16,2560]{1,0:T(8,128)(2,1)S(1)} collective-permute-done((bf16[16,2560]{1,0:T(8,128)(2,1)S(1)}, bf16[16,2560]{1,0:T(8,128)(2,1)S(1)}, u32[]{:S(2)}, u32[]{:S(2)}) %collective-permute-start.108) | collective-permute-done | bytes 81952 | tf_op jit(solution)/shard_map/ppermute | solution.py:292
  367.5 18.7 %collective-permute-start.116 = (bf16[16,2560]{1,0:T(8,128)(2,1)S(1)}, bf16[16,2560]{1,0:T(8,128)(2,1)S(1)}, u32[]{:S(2)}, u32[]{:S(2)}) collective-permute-start(bf16[16,2560]{1,0:T(8,128)(2,1)S(1)} %fusion.12), channel_id=1, source_target_pairs={{0,48},{2,50},{4,52},{6,54},{8,56},{10,58},{12,60},{14,62},{16,32}... | collective-permute-start | bytes 245768 | tf_op jit(solution)/shard_map/ppermute | solution.py:292
  390.2 6.6 %collective-permute-done.117 = bf16[16,2560]{1,0:T(8,128)(2,1)S(1)} collective-permute-done((bf16[16,2560]{1,0:T(8,128)(2,1)S(1)}, bf16[16,2560]{1,0:T(8,128)(2,1)S(1)}, u32[]{:S(2)}, u32[]{:S(2)}) %collective-permute-start.117) | collective-permute-done | bytes 81952 | tf_op jit(solution)/shard_map/ppermute | solution.py:292
  410.7 11.1 %collective-permute-start.125 = (bf16[16,2560]{1,0:T(8,128)(2,1)S(1)}, bf16[16,2560]{1,0:T(8,128)(2,1)S(1)}, u32[]{:S(2)}, u32[]{:S(2)}) collective-permute-start(bf16[16,2560]{1,0:T(8,128)(2,1)S(1)} %fusion.7), channel_id=1, source_target_pairs={{0,16},{2,18},{4,20},{6,22},{8,24},{10,26},{12,28},{14,30},{16,0},... | collective-permute-start | bytes 245768 | tf_op jit(solution)/shard_map/ppermute | solution.py:292
  425.6 5.8 %collective-permute-done.126 = bf16[16,2560]{1,0:T(8,128)(2,1)S(1)} collective-permute-done((bf16[16,2560]{1,0:T(8,128)(2,1)S(1)}, bf16[16,2560]{1,0:T(8,128)(2,1)S(1)}, u32[]{:S(2)}, u32[]{:S(2)}) %collective-permute-start.126) | collective-permute-done | bytes 81952 | tf_op jit(solution)/shard_map/ppermute | solution.py:292
  457.9 9.4 %collective-permute-done.136.refs_13_ = bf16[64,2304]{1,0:T(8,128)(2,1)S(1)} collective-permute-done((bf16[64,2304]{1,0:T(8,128)(2,1)S(1)}, bf16[64,2304]{1,0:T(8,128)(2,1)S(1)}, u32[]{:S(2)}, u32[]{:S(2)}) %collective-permute-start.136) | collective-permute-done | bytes 294944 | tf_op jit(solution)/shard_map/ppermute | solution.py:319
  469.8 5.8 %collective-permute-done.134.refs_11_ = bf16[64,2304]{1,0:T(8,128)(2,1)S(1)} collective-permute-done((bf16[64,2304]{1,0:T(8,128)(2,1)S(1)}, bf16[64,2304]{1,0:T(8,128)(2,1)S(1)}, u32[]{:S(2)}, u32[]{:S(2)}) %collective-permute-start.134) | collective-permute-done | bytes 294944 | tf_op jit(solution)/shard_map/ppermute | solution.py:323
  475.6 6.3 %grad.1 = (f32[3,1280,384]{2,1,0:T(8,128)}, f32[1280,384]{1,0:T(8,128)}) custom-call(s32[4]{0:T(128)S(1)} %add_add_fusion.sc, bf16[64,2048]{1,0:T(8,128)(2,1)S(1)} %get-tuple-element.151.refs_0_, bf16[64,2048]{1,0:T(8,128)(2,1)S(1)} %collective-permute-done.81.refs_1_, bf16[64,2048]{1,0:T(8,128)(2,1)S(1)} %collective-permute-done.82.refs_2_, ...), custom_call_target="tpu_custom_call" | custom-call | tf_op jit(solution)/shard_map/grad/pallas_call | solution.py:363
  (454 shorter events, 300.0 us)
Async XLA Ops:
  21.3 11.0 %collective-permute-start.7 = (bf16[16,2560]{1,0:T(8,128)(2,1)S(1)}, bf16[16,2560]{1,0:T(8,128)(2,1)S(1)}, u32[]{:S(2)}, u32[]{:S(2)}) collective-permute-start(bf16[16,2560]{1,0:T(8,128)(2,1)S(1)} %add_convert_fusion.20), channel_id=1, source_target_pairs={{0,24},{2,26},{4,28},{6,30},{8,16},{10,18},{12,20},{14,22},{16,8},... | collective-permute-start | bytes 245768 | tf_op jit(solution)/shard_map/ppermute | solution.py:292
  44.8 12.0 %collective-permute-start.16 = (bf16[16,2560]{1,0:T(8,128)(2,1)S(1)}, bf16[16,2560]{1,0:T(8,128)(2,1)S(1)}, u32[]{:S(2)}, u32[]{:S(2)}) collective-permute-start(bf16[16,2560]{1,0:T(8,128)(2,1)S(1)} %add_convert_fusion.19), channel_id=1, source_target_pairs={{0,56},{2,58},{4,60},{6,62},{8,48},{10,50},{12,52},{14,54},{16,40}... | collective-permute-start | bytes 245768 | tf_op jit(solution)/shard_map/ppermute | solution.py:292
  99.8 13.3 %collective-permute-start.34 = (bf16[16,2560]{1,0:T(8,128)(2,1)S(1)}, bf16[16,2560]{1,0:T(8,128)(2,1)S(1)}, u32[]{:S(2)}, u32[]{:S(2)}) collective-permute-start(bf16[16,2560]{1,0:T(8,128)(2,1)S(1)} %add_convert_fusion.17), channel_id=1, source_target_pairs={{0,120},{2,122},{4,124},{6,126},{8,112},{10,114},{12,116},{14,118}... | collective-permute-start | bytes 245768 | tf_op jit(solution)/shard_map/ppermute | solution.py:292
  100.0 13.1 %collective-permute-start.33 = (bf16[16,2560]{1,0:T(8,128)(2,1)S(1)}, bf16[16,2560]{1,0:T(8,128)(2,1)S(1)}, u32[]{:S(2)}, u32[]{:S(2)}) collective-permute-start(bf16[16,2560]{1,0:T(8,128)(2,1)S(1)} %add_convert_fusion.17), channel_id=1, source_target_pairs={{0,124},{2,126},{4,112},{6,114},{8,116},{10,118},{12,120},{14,122}... | collective-permute-start | bytes 245768 | tf_op jit(solution)/shard_map/ppermute | solution.py:292
  149.1 21.7 %collective-permute-start.49 = (bf16[16,2560]{1,0:T(8,128)(2,1)S(1)}, bf16[16,2560]{1,0:T(8,128)(2,1)S(1)}, u32[]{:S(2)}, u32[]{:S(2)}) collective-permute-start(bf16[16,2560]{1,0:T(8,128)(2,1)S(1)} %add_convert_fusion.15), channel_id=1, source_target_pairs={{0,48},{2,50},{4,52},{6,54},{8,56},{10,58},{12,60},{14,62},{16,32}... | collective-permute-start | bytes 245768 | tf_op jit(solution)/shard_map/ppermute | solution.py:292
  166.8 10.7 %collective-permute-start.52 = (bf16[16,2560]{1,0:T(8,128)(2,1)S(1)}, bf16[16,2560]{1,0:T(8,128)(2,1)S(1)}, u32[]{:S(2)}, u32[]{:S(2)}) collective-permute-start(bf16[16,2560]{1,0:T(8,128)(2,1)S(1)} %add_convert_fusion.15), channel_id=1, source_target_pairs={{0,56},{2,58},{4,60},{6,62},{8,48},{10,50},{12,52},{14,54},{16,40}... | collective-permute-start | bytes 245768 | tf_op jit(solution)/shard_map/ppermute | solution.py:292
  167.2 10.2 %collective-permute-start.51 = (bf16[16,2560]{1,0:T(8,128)(2,1)S(1)}, bf16[16,2560]{1,0:T(8,128)(2,1)S(1)}, u32[]{:S(2)}, u32[]{:S(2)}) collective-permute-start(bf16[16,2560]{1,0:T(8,128)(2,1)S(1)} %add_convert_fusion.15), channel_id=1, source_target_pairs={{0,60},{2,62},{4,48},{6,50},{8,52},{10,54},{12,56},{14,58},{16,44}... | collective-permute-start | bytes 245768 | tf_op jit(solution)/shard_map/ppermute | solution.py:292
  191.3 12.2 %collective-permute-start.58 = (bf16[16,2560]{1,0:T(8,128)(2,1)S(1)}, bf16[16,2560]{1,0:T(8,128)(2,1)S(1)}, u32[]{:S(2)}, u32[]{:S(2)}) collective-permute-start(bf16[16,2560]{1,0:T(8,128)(2,1)S(1)} %add_convert_fusion.14), channel_id=1, source_target_pairs={{0,16},{2,18},{4,20},{6,22},{8,24},{10,26},{12,28},{14,30},{16,0},... | collective-permute-start | bytes 245768 | tf_op jit(solution)/shard_map/ppermute | solution.py:292
  246.5 14.2 %collective-permute-start.82 = (bf16[64,2048]{1,0:T(8,128)(2,1)S(1)}, bf16[64,2048]{1,0:T(8,128)(2,1)S(1)}, u32[]{:S(2)}, u32[]{:S(2)}) collective-permute-start(bf16[64,2048]{1,0:T(8,128)(2,1)S(1)} %get-tuple-element.297), channel_id=1, source_target_pairs={{0,112},{16,96},{32,80},{48,64},{64,48},{80,32},{96,16},{112,0},{1... | collective-permute-start | bytes 786440 | tf_op jit(solution)/shard_map/ppermute | solution.py:319
  247.4 14.1 %collective-permute-start.83 = (bf16[64,2048]{1,0:T(8,128)(2,1)S(1)}, bf16[64,2048]{1,0:T(8,128)(2,1)S(1)}, u32[]{:S(2)}, u32[]{:S(2)}) collective-permute-start(bf16[64,2048]{1,0:T(8,128)(2,1)S(1)} %get-tuple-element.298), channel_id=1, source_target_pairs={{0,113},{16,97},{32,81},{48,65},{64,49},{80,33},{96,17},{112,1},{1... | collective-permute-start | bytes 786440 | tf_op jit(solution)/shard_map/ppermute | solution.py:319
  265.6 16.3 %collective-permute-start.84 = (bf16[192,1280]{1,0:T(8,128)(2,1)S(1)}, bf16[192,1280]{1,0:T(8,128)(2,1)S(1)}, u32[]{:S(2)}, u32[]{:S(2)}) collective-permute-start(bf16[192,1280]{1,0:T(8,128)(2,1)S(1)} %pad_maximum_fusion.4), channel_id=1, source_target_pairs={{0,2},{2,0},{4,6},{6,4},{8,10},{10,8},{12,14},{14,12},{16,18},{18,... | collective-permute-start | bytes 1474568 | tf_op jit(solution)/shard_map/ppermute | solution.py:292
  268.5 12.0 %collective-permute-start.79 = (bf16[16,2560]{1,0:T(8,128)(2,1)S(1)}, bf16[16,2560]{1,0:T(8,128)(2,1)S(1)}, u32[]{:S(2)}, u32[]{:S(2)}) collective-permute-start(bf16[16,2560]{1,0:T(8,128)(2,1)S(1)} %fusion.32), channel_id=1, source_target_pairs={{0,56},{2,58},{4,60},{6,62},{8,48},{10,50},{12,52},{14,54},{16,40}... | collective-permute-start | bytes 245768 | tf_op jit(solution)/shard_map/ppermute | solution.py:292
  270.3 10.2 %collective-permute-start.78 = (bf16[16,2560]{1,0:T(8,128)(2,1)S(1)}, bf16[16,2560]{1,0:T(8,128)(2,1)S(1)}, u32[]{:S(2)}, u32[]{:S(2)}) collective-permute-start(bf16[16,2560]{1,0:T(8,128)(2,1)S(1)} %fusion.32), channel_id=1, source_target_pairs={{0,60},{2,62},{4,48},{6,50},{8,52},{10,54},{12,56},{14,58},{16,44}... | collective-permute-start | bytes 245768 | tf_op jit(solution)/shard_map/ppermute | solution.py:292
  317.2 13.4 %collective-permute-start.101 = (bf16[16,2560]{1,0:T(8,128)(2,1)S(1)}, bf16[16,2560]{1,0:T(8,128)(2,1)S(1)}, u32[]{:S(2)}, u32[]{:S(2)}) collective-permute-start(bf16[16,2560]{1,0:T(8,128)(2,1)S(1)} %fusion.22), channel_id=1, source_target_pairs={{0,120},{2,122},{4,124},{6,126},{8,112},{10,114},{12,116},{14,118}... | collective-permute-start | bytes 245768 | tf_op jit(solution)/shard_map/ppermute | solution.py:292
  319.9 10.7 %collective-permute-start.100 = (bf16[16,2560]{1,0:T(8,128)(2,1)S(1)}, bf16[16,2560]{1,0:T(8,128)(2,1)S(1)}, u32[]{:S(2)}, u32[]{:S(2)}) collective-permute-start(bf16[16,2560]{1,0:T(8,128)(2,1)S(1)} %fusion.22), channel_id=1, source_target_pairs={{0,124},{2,126},{4,112},{6,114},{8,116},{10,118},{12,120},{14,122}... | collective-permute-start | bytes 245768 | tf_op jit(solution)/shard_map/ppermute | solution.py:292
  367.5 22.8 %collective-permute-start.116 = (bf16[16,2560]{1,0:T(8,128)(2,1)S(1)}, bf16[16,2560]{1,0:T(8,128)(2,1)S(1)}, u32[]{:S(2)}, u32[]{:S(2)}) collective-permute-start(bf16[16,2560]{1,0:T(8,128)(2,1)S(1)} %fusion.12), channel_id=1, source_target_pairs={{0,48},{2,50},{4,52},{6,54},{8,56},{10,58},{12,60},{14,62},{16,32}... | collective-permute-start | bytes 245768 | tf_op jit(solution)/shard_map/ppermute | solution.py:292
  386.2 10.7 %collective-permute-start.119 = (bf16[16,2560]{1,0:T(8,128)(2,1)S(1)}, bf16[16,2560]{1,0:T(8,128)(2,1)S(1)}, u32[]{:S(2)}, u32[]{:S(2)}) collective-permute-start(bf16[16,2560]{1,0:T(8,128)(2,1)S(1)} %fusion.12), channel_id=1, source_target_pairs={{0,56},{2,58},{4,60},{6,62},{8,48},{10,50},{12,52},{14,54},{16,40}... | collective-permute-start | bytes 245768 | tf_op jit(solution)/shard_map/ppermute | solution.py:292
  386.6 10.2 %collective-permute-start.118 = (bf16[16,2560]{1,0:T(8,128)(2,1)S(1)}, bf16[16,2560]{1,0:T(8,128)(2,1)S(1)}, u32[]{:S(2)}, u32[]{:S(2)}) collective-permute-start(bf16[16,2560]{1,0:T(8,128)(2,1)S(1)} %fusion.12), channel_id=1, source_target_pairs={{0,60},{2,62},{4,48},{6,50},{8,52},{10,54},{12,56},{14,58},{16,44}... | collective-permute-start | bytes 245768 | tf_op jit(solution)/shard_map/ppermute | solution.py:292
  410.7 14.9 %collective-permute-start.125 = (bf16[16,2560]{1,0:T(8,128)(2,1)S(1)}, bf16[16,2560]{1,0:T(8,128)(2,1)S(1)}, u32[]{:S(2)}, u32[]{:S(2)}) collective-permute-start(bf16[16,2560]{1,0:T(8,128)(2,1)S(1)} %fusion.7), channel_id=1, source_target_pairs={{0,16},{2,18},{4,20},{6,22},{8,24},{10,26},{12,28},{14,30},{16,0},... | collective-permute-start | bytes 245768 | tf_op jit(solution)/shard_map/ppermute | solution.py:292
  436.6 13.0 %collective-permute-start.132 = (bf16[64,1280]{1,0:T(8,128)(2,1)S(1)}, bf16[64,1280]{1,0:T(8,128)(2,1)S(1)}, u32[]{:S(2)}, u32[]{:S(2)}) collective-permute-start(bf16[64,1280]{1,0:T(8,128)(2,1)S(1)} %get-tuple-element.218), channel_id=1, source_target_pairs={{0,113},{16,97},{32,81},{48,65},{64,49},{80,33},{96,17},{112,1},{1... | collective-permute-start | bytes 491528 | tf_op jit(solution)/shard_map/ppermute | solution.py:319
  438.1 11.4 %collective-permute-start.131 = (bf16[64,1280]{1,0:T(8,128)(2,1)S(1)}, bf16[64,1280]{1,0:T(8,128)(2,1)S(1)}, u32[]{:S(2)}, u32[]{:S(2)}) collective-permute-start(bf16[64,1280]{1,0:T(8,128)(2,1)S(1)} %get-tuple-element.219), channel_id=1, source_target_pairs={{0,112},{16,96},{32,80},{48,64},{64,48},{80,32},{96,16},{112,0},{1... | collective-permute-start | bytes 491528 | tf_op jit(solution)/shard_map/ppermute | solution.py:319
  451.8 15.5 %collective-permute-start.136 = (bf16[64,2304]{1,0:T(8,128)(2,1)S(1)}, bf16[64,2304]{1,0:T(8,128)(2,1)S(1)}, u32[]{:S(2)}, u32[]{:S(2)}) collective-permute-start(bf16[64,2304]{1,0:T(8,128)(2,1)S(1)} %get-tuple-element.249), channel_id=1, source_target_pairs={{0,113},{16,97},{32,81},{48,65},{64,49},{80,33},{96,17},{112,1},{1... | collective-permute-start | bytes 884744 | tf_op jit(solution)/shard_map/ppermute | solution.py:319
  453.8 16.0 %collective-permute-start.135 = (bf16[64,2304]{1,0:T(8,128)(2,1)S(1)}, bf16[64,2304]{1,0:T(8,128)(2,1)S(1)}, u32[]{:S(2)}, u32[]{:S(2)}) collective-permute-start(bf16[64,2304]{1,0:T(8,128)(2,1)S(1)} %get-tuple-element.249), channel_id=1, source_target_pairs={{0,112},{16,96},{32,80},{48,64},{64,48},{80,32},{96,16},{112,0},{1... | collective-permute-start | bytes 884744 | tf_op jit(solution)/shard_map/ppermute | solution.py:319
  454.1 21.6 %collective-permute-start.134 = (bf16[64,2304]{1,0:T(8,128)(2,1)S(1)}, bf16[64,2304]{1,0:T(8,128)(2,1)S(1)}, u32[]{:S(2)}, u32[]{:S(2)}) collective-permute-start(bf16[64,2304]{1,0:T(8,128)(2,1)S(1)} %get-tuple-element.250.refs_10_), channel_id=1, source_target_pairs={{0,1},{1,0},{2,3},{3,2},{4,5},{5,4},{6,7},{7,6},{8,9},{9,8},{10,11... | collective-permute-start | bytes 884744 | tf_op jit(solution)/shard_map/ppermute | solution.py:323
  (120 other events, 657.4 us)

commit v4 on v3

--- a/solution.py
+++ b/solution.py
@@ -127,9 +127,9 @@
             pltpu.make_async_copy(qkv_i.at[d], qkv, ssem.at[0]),
             pltpu.make_async_copy(prob_i.at[d], prob, ssem.at[1]),
         ]
-        start_weights(d, down, up, held, wsem)
         for load in loads:
             load.start()
+        start_weights(d, down, up, held, wsem)
         for ref, half in ((own, c), (oth, 1 - c)):
             for i in range(4):
                 dy[pl.ds(piece_rows(z, i, half), 16), :] = ref[16 * i : 16 * i + 16, :]

time: 491 us -> 490 us (level)
  transfers between devices with their start and end apart: 137 -> 137, of which waited for: 81 -> 80; matrix products, arithmetic and copies ran while one was open for 0% -> 0% of each run, Pallas kernels for 1% -> 1%
where the time goes in v4:
time: 490 us; the launch traced here: 481 us
  starting transfers between devices  228 us (47%)
  waiting for transfers between devices  203 us (41%)
  Pallas kernels  37.1 us (8%)
  other arithmetic  7.85 us (2%)
    ppermute x128, starting transfers between devices, permute(): return lax.ppermute(x, AXES, pairs)  210 us
    ppermute x128, waiting for transfers between devices, permute(): return lax.ppermute(x, AXES, pairs)  177 us
    ppermute x6, waiting for transfers between devices, mirror(): return lax.ppermute(a, ('pipe', 'dp'), pairs)  18.9 us
    pallas_call x8, Pallas kernels, front_call(): pl.pallas_call(functools.partial(front_kernel, last), out_shape=halves +...  15.9 us
    pallas_call x8, Pallas kernels, back_call(): pl.pallas_call(functools.partial(back_kernel, last), out_shape=halves + [...  15 us
  transfers between devices with their start and end apart: 137, of which 80 were waited for; matrix products, arithmetic and copies ran while one was open for 0% of the time, Pallas kernels for 1%

profile of v4, /device:TPU:1, one launch (start us, length us, event | category | flops | bytes accessed | tf_op | source)
XLA Modules:
  0.0 481.0 jit_solution(4995135601914611356)
XLA Ops:
  3.8 5.8 %front.8 = (bf16[64,2560]{1,0:T(8,128)(2,1)S(1)}, bf16[64,2560]{1,0:T(8,128)(2,1)S(1)}, bf16[2,128,2560]{2,1,0:T(8,128)(2,1)}, bf16[2,3,128,384]{3,2,1,0:T(8,128...) custom-call(s32[4]{0:T(128)S(1)} %add_add_fusion.sc, ...), custom_call_target="tpu_custom_call", output_to_operand_aliasing={{2}: (9, {}), {3}: (10, {}), {4}: (11, {}), {5}: (12, {})} | custom-call | flops 1006632960 | bytes 7864320 | tf_op jit(solution)/shard_map/front/pallas_call | solution.py:207
  27.0 5.3 %collective-permute-done.5 = bf16[16,2560]{1,0:T(8,128)(2,1)S(1)} collective-permute-done((bf16[16,2560]{1,0:T(8,128)(2,1)S(1)}, bf16[16,2560]{1,0:T(8,128)(2,1)S(1)}, u32[]{:S(2)}, u32[]{:S(2)}) %collective-permute-start.5) | collective-permute-done | bytes 81952 | tf_op jit(solution)/shard_map/ppermute | solution.py:292
  77.2 6.2 %collective-permute-done.23 = bf16[16,2560]{1,0:T(8,128)(2,1)S(1)} collective-permute-done((bf16[16,2560]{1,0:T(8,128)(2,1)S(1)}, bf16[16,2560]{1,0:T(8,128)(2,1)S(1)}, u32[]{:S(2)}, u32[]{:S(2)}) %collective-permute-start.23) | collective-permute-done | bytes 81952 | tf_op jit(solution)/shard_map/ppermute | solution.py:292
  100.0 5.6 %collective-permute-start.33 = (bf16[16,2560]{1,0:T(8,128)(2,1)S(1)}, bf16[16,2560]{1,0:T(8,128)(2,1)S(1)}, u32[]{:S(2)}, u32[]{:S(2)}) collective-permute-start(bf16[16,2560]{1,0:T(8,128)(2,1)S(1)} %add_convert_fusion.17), channel_id=1, source_target_pairs={{0,124},{2,126},{4,112},{6,114},{8,116},{10,118},{12,120},{14,122}... | collective-permute-start | bytes 245768 | tf_op jit(solution)/shard_map/ppermute | solution.py:292
  105.6 7.5 %collective-permute-done.32 = bf16[16,2560]{1,0:T(8,128)(2,1)S(1)} collective-permute-done((bf16[16,2560]{1,0:T(8,128)(2,1)S(1)}, bf16[16,2560]{1,0:T(8,128)(2,1)S(1)}, u32[]{:S(2)}, u32[]{:S(2)}) %collective-permute-start.32) | collective-permute-done | bytes 81952 | tf_op jit(solution)/shard_map/ppermute | solution.py:292
  149.1 17.6 %collective-permute-start.49 = (bf16[16,2560]{1,0:T(8,128)(2,1)S(1)}, bf16[16,2560]{1,0:T(8,128)(2,1)S(1)}, u32[]{:S(2)}, u32[]{:S(2)}) collective-permute-start(bf16[16,2560]{1,0:T(8,128)(2,1)S(1)} %add_convert_fusion.15), channel_id=1, source_target_pairs={{0,48},{2,50},{4,52},{6,54},{8,56},{10,58},{12,60},{14,62},{16,32}... | collective-permute-start | bytes 245768 | tf_op jit(solution)/shard_map/ppermute | solution.py:292
  170.8 6.6 %collective-permute-done.50 = bf16[16,2560]{1,0:T(8,128)(2,1)S(1)} collective-permute-done((bf16[16,2560]{1,0:T(8,128)(2,1)S(1)}, bf16[16,2560]{1,0:T(8,128)(2,1)S(1)}, u32[]{:S(2)}, u32[]{:S(2)}) %collective-permute-start.50) | collective-permute-done | bytes 81952 | tf_op jit(solution)/shard_map/ppermute | solution.py:292
  191.3 8.3 %collective-permute-start.58 = (bf16[16,2560]{1,0:T(8,128)(2,1)S(1)}, bf16[16,2560]{1,0:T(8,128)(2,1)S(1)}, u32[]{:S(2)}, u32[]{:S(2)}) collective-permute-start(bf16[16,2560]{1,0:T(8,128)(2,1)S(1)} %add_convert_fusion.14), channel_id=1, source_target_pairs={{0,16},{2,18},{4,20},{6,22},{8,24},{10,26},{12,28},{14,30},{16,0},... | collective-permute-start | bytes 245768 | tf_op jit(solution)/shard_map/ppermute | solution.py:292
  203.6 5.7 %collective-permute-done.59 = bf16[16,2560]{1,0:T(8,128)(2,1)S(1)} collective-permute-done((bf16[16,2560]{1,0:T(8,128)(2,1)S(1)}, bf16[16,2560]{1,0:T(8,128)(2,1)S(1)}, u32[]{:S(2)}, u32[]{:S(2)}) %collective-permute-start.59) | collective-permute-done | bytes 81952 | tf_op jit(solution)/shard_map/ppermute | solution.py:292
  212.8 5.7 %front.15 = (bf16[2,128,2560]{2,1,0:T(8,128)(2,1)}, bf16[2,3,128,384]{3,2,1,0:T(8,128)(2,1)}, f32[2,3,128,128]{3,2,1,0:T(8,128)}, bf16[2,64,768]{2,1,0:T(8,128)(2,1)}) custom-call(s32[4]{0:T(128)S(1)} %add_add_fusion.7.sc, ...), custom_call_target="tpu_custom_call", output_to_operand_aliasing={{0}: (9, {}), {1}: (10, {}), {2}: (11, {}), {3}: (12, {})} | custom-call | flops 1006632960 | bytes 7864320 | tf_op jit(solution)/shard_map/front/pallas_call | solution.py:207
  218.5 6.4 %back.8 = (bf16[64,2560]{1,0:T(8,128)(2,1)S(1)}, bf16[64,2560]{1,0:T(8,128)(2,1)S(1)}, bf16[2,128,2560]{2,1,0:T(8,128)(2,1)}, bf16[2,64,2304]{2,1,0:T(8,128)(2,1)}) custom-call(s32[4]{0:T(128)S(1)} %add_add_fusion.7.sc, bf16[64,2560]{1,0:T(8,128)(2,1)S(1)} %get-tuple-element.313.own, ...), custom_call_target="tpu_custom_call", output_to_operand_aliasing={{2}: (9, {}), {3}: (10, {})} | custom-call | flops 1006632960 | bytes 7864320 | tf_op jit(solution)/shard_map/back/pallas_call | solution.py:236
  237.9 5.5 %collective-permute-done.68 = bf16[16,2560]{1,0:T(8,128)(2,1)S(1)} collective-permute-done((bf16[16,2560]{1,0:T(8,128)(2,1)S(1)}, bf16[16,2560]{1,0:T(8,128)(2,1)S(1)}, u32[]{:S(2)}, u32[]{:S(2)}) %collective-permute-start.68) | collective-permute-done | bytes 81952 | tf_op jit(solution)/shard_map/ppermute | solution.py:292
  272.5 6.6 %collective-permute-done.77 = bf16[16,2560]{1,0:T(8,128)(2,1)S(1)} collective-permute-done((bf16[16,2560]{1,0:T(8,128)(2,1)S(1)}, bf16[16,2560]{1,0:T(8,128)(2,1)S(1)}, u32[]{:S(2)}, u32[]{:S(2)}) %collective-permute-start.77) | collective-permute-done | bytes 81952 | tf_op jit(solution)/shard_map/ppermute | solution.py:292
  295.4 5.6 %collective-permute-done.90 = bf16[16,2560]{1,0:T(8,128)(2,1)S(1)} collective-permute-done((bf16[16,2560]{1,0:T(8,128)(2,1)S(1)}, bf16[16,2560]{1,0:T(8,128)(2,1)S(1)}, u32[]{:S(2)}, u32[]{:S(2)}) %collective-permute-start.90) | collective-permute-done | bytes 81952 | tf_op jit(solution)/shard_map/ppermute | solution.py:292
  323.0 6.7 %collective-permute-done.99 = bf16[16,2560]{1,0:T(8,128)(2,1)S(1)} collective-permute-done((bf16[16,2560]{1,0:T(8,128)(2,1)S(1)}, bf16[16,2560]{1,0:T(8,128)(2,1)S(1)}, u32[]{:S(2)}, u32[]{:S(2)}) %collective-permute-start.99) | collective-permute-done | bytes 81952 | tf_op jit(solution)/shard_map/ppermute | solution.py:292
  347.0 6.2 %collective-permute-done.108 = bf16[16,2560]{1,0:T(8,128)(2,1)S(1)} collective-permute-done((bf16[16,2560]{1,0:T(8,128)(2,1)S(1)}, bf16[16,2560]{1,0:T(8,128)(2,1)S(1)}, u32[]{:S(2)}, u32[]{:S(2)}) %collective-permute-start.108) | collective-permute-done | bytes 81952 | tf_op jit(solution)/shard_map/ppermute | solution.py:292
  365.9 20.6 %collective-permute-start.116 = (bf16[16,2560]{1,0:T(8,128)(2,1)S(1)}, bf16[16,2560]{1,0:T(8,128)(2,1)S(1)}, u32[]{:S(2)}, u32[]{:S(2)}) collective-permute-start(bf16[16,2560]{1,0:T(8,128)(2,1)S(1)} %fusion.12), channel_id=1, source_target_pairs={{0,48},{2,50},{4,52},{6,54},{8,56},{10,58},{12,60},{14,62},{16,32}... | collective-permute-start | bytes 245768 | tf_op jit(solution)/shard_map/ppermute | solution.py:292
  390.5 6.6 %collective-permute-done.117 = bf16[16,2560]{1,0:T(8,128)(2,1)S(1)} collective-permute-done((bf16[16,2560]{1,0:T(8,128)(2,1)S(1)}, bf16[16,2560]{1,0:T(8,128)(2,1)S(1)}, u32[]{:S(2)}, u32[]{:S(2)}) %collective-permute-start.117) | collective-permute-done | bytes 81952 | tf_op jit(solution)/shard_map/ppermute | solution.py:292
  410.9 10.8 %collective-permute-start.125 = (bf16[16,2560]{1,0:T(8,128)(2,1)S(1)}, bf16[16,2560]{1,0:T(8,128)(2,1)S(1)}, u32[]{:S(2)}, u32[]{:S(2)}) collective-permute-start(bf16[16,2560]{1,0:T(8,128)(2,1)S(1)} %fusion.7), channel_id=1, source_target_pairs={{0,16},{2,18},{4,20},{6,22},{8,24},{10,26},{12,28},{14,30},{16,0},... | collective-permute-start | bytes 245768 | tf_op jit(solution)/shard_map/ppermute | solution.py:292
  425.5 5.8 %collective-permute-done.126 = bf16[16,2560]{1,0:T(8,128)(2,1)S(1)} collective-permute-done((bf16[16,2560]{1,0:T(8,128)(2,1)S(1)}, bf16[16,2560]{1,0:T(8,128)(2,1)S(1)}, u32[]{:S(2)}, u32[]{:S(2)}) %collective-permute-start.126) | collective-permute-done | bytes 81952 | tf_op jit(solution)/shard_map/ppermute | solution.py:292
  442.8 4.9 %back.15 = (bf16[2,128,2560]{2,1,0:T(8,128)(2,1)}, bf16[2,64,2304]{2,1,0:T(8,128)(2,1)}) custom-call(s32[4]{0:T(128)S(1)} %add_add_fusion.sc, bf16[64,2560]{1,0:T(8,128)(2,1)S(1)} %constant_dynamic-update-slice_fusion.52.own, bf16[64,2560]{1,0:T(8,128)(2,1)S(1)} %collective-permute-done.129.oth, ...), custom_call_target="tpu_custom_call", output_to_operand_aliasing={{0}: (9, {}), {1}: (10, {})} | custom-call | flops 1006632960 | bytes 7864320 | tf_op jit(solution)/shard_map/back/pallas_call | solution.py:236
  454.2 5.0 %collective-permute-start.134 = (bf16[64,2304]{1,0:T(8,128)(2,1)S(1)}, bf16[64,2304]{1,0:T(8,128)(2,1)S(1)}, u32[]{:S(2)}, u32[]{:S(2)}) collective-permute-start(bf16[64,2304]{1,0:T(8,128)(2,1)S(1)} %get-tuple-element.250.refs_10_), channel_id=1, source_target_pairs={{0,1},{1,0},{2,3},{3,2},{4,5},{5,4},{6,7},{7,6},{8,9},{9,8},{10,11... | collective-permute-start | bytes 884744 | tf_op jit(solution)/shard_map/ppermute | solution.py:323
  459.2 13.1 %collective-permute-done.136.refs_13_ = bf16[64,2304]{1,0:T(8,128)(2,1)S(1)} collective-permute-done((bf16[64,2304]{1,0:T(8,128)(2,1)S(1)}, bf16[64,2304]{1,0:T(8,128)(2,1)S(1)}, u32[]{:S(2)}, u32[]{:S(2)}) %collective-permute-start.136) | collective-permute-done | bytes 294944 | tf_op jit(solution)/shard_map/ppermute | solution.py:319
  474.3 6.3 %grad.1 = (f32[3,1280,384]{2,1,0:T(8,128)}, f32[1280,384]{1,0:T(8,128)}) custom-call(s32[4]{0:T(128)S(1)} %add_add_fusion.sc, bf16[64,2048]{1,0:T(8,128)(2,1)S(1)} %get-tuple-element.151.refs_0_, bf16[64,2048]{1,0:T(8,128)(2,1)S(1)} %collective-permute-done.81.refs_1_, bf16[64,2048]{1,0:T(8,128)(2,1)S(1)} %collective-permute-done.82.refs_2_, ...), custom_call_target="tpu_custom_call" | custom-call | tf_op jit(solution)/shard_map/grad/pallas_call | solution.py:363
  (454 shorter events, 293.9 us)
Async XLA Ops:
  21.3 11.0 %collective-permute-start.7 = (bf16[16,2560]{1,0:T(8,128)(2,1)S(1)}, bf16[16,2560]{1,0:T(8,128)(2,1)S(1)}, u32[]{:S(2)}, u32[]{:S(2)}) collective-permute-start(bf16[16,2560]{1,0:T(8,128)(2,1)S(1)} %add_convert_fusion.20), channel_id=1, source_target_pairs={{0,24},{2,26},{4,28},{6,30},{8,16},{10,18},{12,20},{14,22},{16,8},... | collective-permute-start | bytes 245768 | tf_op jit(solution)/shard_map/ppermute | solution.py:292
  44.8 12.0 %collective-permute-start.16 = (bf16[16,2560]{1,0:T(8,128)(2,1)S(1)}, bf16[16,2560]{1,0:T(8,128)(2,1)S(1)}, u32[]{:S(2)}, u32[]{:S(2)}) collective-permute-start(bf16[16,2560]{1,0:T(8,128)(2,1)S(1)} %add_convert_fusion.19), channel_id=1, source_target_pairs={{0,56},{2,58},{4,60},{6,62},{8,48},{10,50},{12,52},{14,54},{16,40}... | collective-permute-start | bytes 245768 | tf_op jit(solution)/shard_map/ppermute | solution.py:292
  99.8 13.3 %collective-permute-start.34 = (bf16[16,2560]{1,0:T(8,128)(2,1)S(1)}, bf16[16,2560]{1,0:T(8,128)(2,1)S(1)}, u32[]{:S(2)}, u32[]{:S(2)}) collective-permute-start(bf16[16,2560]{1,0:T(8,128)(2,1)S(1)} %add_convert_fusion.17), channel_id=1, source_target_pairs={{0,120},{2,122},{4,124},{6,126},{8,112},{10,114},{12,116},{14,118}... | collective-permute-start | bytes 245768 | tf_op jit(solution)/shard_map/ppermute | solution.py:292
  100.0 13.1 %collective-permute-start.33 = (bf16[16,2560]{1,0:T(8,128)(2,1)S(1)}, bf16[16,2560]{1,0:T(8,128)(2,1)S(1)}, u32[]{:S(2)}, u32[]{:S(2)}) collective-permute-start(bf16[16,2560]{1,0:T(8,128)(2,1)S(1)} %add_convert_fusion.17), channel_id=1, source_target_pairs={{0,124},{2,126},{4,112},{6,114},{8,116},{10,118},{12,120},{14,122}... | collective-permute-start | bytes 245768 | tf_op jit(solution)/shard_map/ppermute | solution.py:292
  149.1 21.7 %collective-permute-start.49 = (bf16[16,2560]{1,0:T(8,128)(2,1)S(1)}, bf16[16,2560]{1,0:T(8,128)(2,1)S(1)}, u32[]{:S(2)}, u32[]{:S(2)}) collective-permute-start(bf16[16,2560]{1,0:T(8,128)(2,1)S(1)} %add_convert_fusion.15), channel_id=1, source_target_pairs={{0,48},{2,50},{4,52},{6,54},{8,56},{10,58},{12,60},{14,62},{16,32}... | collective-permute-start | bytes 245768 | tf_op jit(solution)/shard_map/ppermute | solution.py:292
  166.8 10.7 %collective-permute-start.52 = (bf16[16,2560]{1,0:T(8,128)(2,1)S(1)}, bf16[16,2560]{1,0:T(8,128)(2,1)S(1)}, u32[]{:S(2)}, u32[]{:S(2)}) collective-permute-start(bf16[16,2560]{1,0:T(8,128)(2,1)S(1)} %add_convert_fusion.15), channel_id=1, source_target_pairs={{0,56},{2,58},{4,60},{6,62},{8,48},{10,50},{12,52},{14,54},{16,40}... | collective-permute-start | bytes 245768 | tf_op jit(solution)/shard_map/ppermute | solution.py:292
  167.2 10.2 %collective-permute-start.51 = (bf16[16,2560]{1,0:T(8,128)(2,1)S(1)}, bf16[16,2560]{1,0:T(8,128)(2,1)S(1)}, u32[]{:S(2)}, u32[]{:S(2)}) collective-permute-start(bf16[16,2560]{1,0:T(8,128)(2,1)S(1)} %add_convert_fusion.15), channel_id=1, source_target_pairs={{0,60},{2,62},{4,48},{6,50},{8,52},{10,54},{12,56},{14,58},{16,44}... | collective-permute-start | bytes 245768 | tf_op jit(solution)/shard_map/ppermute | solution.py:292
  191.3 12.2 %collective-permute-start.58 = (bf16[16,2560]{1,0:T(8,128)(2,1)S(1)}, bf16[16,2560]{1,0:T(8,128)(2,1)S(1)}, u32[]{:S(2)}, u32[]{:S(2)}) collective-permute-start(bf16[16,2560]{1,0:T(8,128)(2,1)S(1)} %add_convert_fusion.14), channel_id=1, source_target_pairs={{0,16},{2,18},{4,20},{6,22},{8,24},{10,26},{12,28},{14,30},{16,0},... | collective-permute-start | bytes 245768 | tf_op jit(solution)/shard_map/ppermute | solution.py:292
  245.9 13.4 %collective-permute-start.82 = (bf16[64,2048]{1,0:T(8,128)(2,1)S(1)}, bf16[64,2048]{1,0:T(8,128)(2,1)S(1)}, u32[]{:S(2)}, u32[]{:S(2)}) collective-permute-start(bf16[64,2048]{1,0:T(8,128)(2,1)S(1)} %get-tuple-element.297), channel_id=1, source_target_pairs={{0,112},{16,96},{32,80},{48,64},{64,48},{80,32},{96,16},{112,0},{1... | collective-permute-start | bytes 786440 | tf_op jit(solution)/shard_map/ppermute | solution.py:319
  247.4 13.6 %collective-permute-start.83 = (bf16[64,2048]{1,0:T(8,128)(2,1)S(1)}, bf16[64,2048]{1,0:T(8,128)(2,1)S(1)}, u32[]{:S(2)}, u32[]{:S(2)}) collective-permute-start(bf16[64,2048]{1,0:T(8,128)(2,1)S(1)} %get-tuple-element.298), channel_id=1, source_target_pairs={{0,113},{16,97},{32,81},{48,65},{64,49},{80,33},{96,17},{112,1},{1... | collective-permute-start | bytes 786440 | tf_op jit(solution)/shard_map/ppermute | solution.py:319
  252.2 10.9 %collective-permute-start.81 = (bf16[64,2048]{1,0:T(8,128)(2,1)S(1)}, bf16[64,2048]{1,0:T(8,128)(2,1)S(1)}, u32[]{:S(2)}, u32[]{:S(2)}) collective-permute-start(bf16[64,2048]{1,0:T(8,128)(2,1)S(1)} %get-tuple-element.296), channel_id=1, source_target_pairs={{0,1},{1,0},{2,3},{3,2},{4,5},{5,4},{6,7},{7,6},{8,9},{9,8},{10,11... | collective-permute-start | bytes 786440 | tf_op jit(solution)/shard_map/ppermute | solution.py:323
  264.2 16.2 %collective-permute-start.84 = (bf16[192,1280]{1,0:T(8,128)(2,1)S(1)}, bf16[192,1280]{1,0:T(8,128)(2,1)S(1)}, u32[]{:S(2)}, u32[]{:S(2)}) collective-permute-start(bf16[192,1280]{1,0:T(8,128)(2,1)S(1)} %pad_maximum_fusion.4), channel_id=1, source_target_pairs={{0,2},{2,0},{4,6},{6,4},{8,10},{10,8},{12,14},{14,12},{16,18},{18,... | collective-permute-start | bytes 1474568 | tf_op jit(solution)/shard_map/ppermute | solution.py:292
  267.1 12.0 %collective-permute-start.79 = (bf16[16,2560]{1,0:T(8,128)(2,1)S(1)}, bf16[16,2560]{1,0:T(8,128)(2,1)S(1)}, u32[]{:S(2)}, u32[]{:S(2)}) collective-permute-start(bf16[16,2560]{1,0:T(8,128)(2,1)S(1)} %fusion.32), channel_id=1, source_target_pairs={{0,56},{2,58},{4,60},{6,62},{8,48},{10,50},{12,52},{14,54},{16,40}... | collective-permute-start | bytes 245768 | tf_op jit(solution)/shard_map/ppermute | solution.py:292
  316.1 13.6 %collective-permute-start.101 = (bf16[16,2560]{1,0:T(8,128)(2,1)S(1)}, bf16[16,2560]{1,0:T(8,128)(2,1)S(1)}, u32[]{:S(2)}, u32[]{:S(2)}) collective-permute-start(bf16[16,2560]{1,0:T(8,128)(2,1)S(1)} %fusion.22), channel_id=1, source_target_pairs={{0,120},{2,122},{4,124},{6,126},{8,112},{10,114},{12,116},{14,118}... | collective-permute-start | bytes 245768 | tf_op jit(solution)/shard_map/ppermute | solution.py:292
  318.5 11.2 %collective-permute-start.100 = (bf16[16,2560]{1,0:T(8,128)(2,1)S(1)}, bf16[16,2560]{1,0:T(8,128)(2,1)S(1)}, u32[]{:S(2)}, u32[]{:S(2)}) collective-permute-start(bf16[16,2560]{1,0:T(8,128)(2,1)S(1)} %fusion.22), channel_id=1, source_target_pairs={{0,124},{2,126},{4,112},{6,114},{8,116},{10,118},{12,120},{14,122}... | collective-permute-start | bytes 245768 | tf_op jit(solution)/shard_map/ppermute | solution.py:292
  365.9 24.6 %collective-permute-start.116 = (bf16[16,2560]{1,0:T(8,128)(2,1)S(1)}, bf16[16,2560]{1,0:T(8,128)(2,1)S(1)}, u32[]{:S(2)}, u32[]{:S(2)}) collective-permute-start(bf16[16,2560]{1,0:T(8,128)(2,1)S(1)} %fusion.12), channel_id=1, source_target_pairs={{0,48},{2,50},{4,52},{6,54},{8,56},{10,58},{12,60},{14,62},{16,32}... | collective-permute-start | bytes 245768 | tf_op jit(solution)/shard_map/ppermute | solution.py:292
  386.4 10.7 %collective-permute-start.119 = (bf16[16,2560]{1,0:T(8,128)(2,1)S(1)}, bf16[16,2560]{1,0:T(8,128)(2,1)S(1)}, u32[]{:S(2)}, u32[]{:S(2)}) collective-permute-start(bf16[16,2560]{1,0:T(8,128)(2,1)S(1)} %fusion.12), channel_id=1, source_target_pairs={{0,56},{2,58},{4,60},{6,62},{8,48},{10,50},{12,52},{14,54},{16,40}... | collective-permute-start | bytes 245768 | tf_op jit(solution)/shard_map/ppermute | solution.py:292
  410.9 14.5 %collective-permute-start.125 = (bf16[16,2560]{1,0:T(8,128)(2,1)S(1)}, bf16[16,2560]{1,0:T(8,128)(2,1)S(1)}, u32[]{:S(2)}, u32[]{:S(2)}) collective-permute-start(bf16[16,2560]{1,0:T(8,128)(2,1)S(1)} %fusion.7), channel_id=1, source_target_pairs={{0,16},{2,18},{4,20},{6,22},{8,24},{10,26},{12,28},{14,30},{16,0},... | collective-permute-start | bytes 245768 | tf_op jit(solution)/shard_map/ppermute | solution.py:292
  436.5 12.2 %collective-permute-start.132 = (bf16[64,1280]{1,0:T(8,128)(2,1)S(1)}, bf16[64,1280]{1,0:T(8,128)(2,1)S(1)}, u32[]{:S(2)}, u32[]{:S(2)}) collective-permute-start(bf16[64,1280]{1,0:T(8,128)(2,1)S(1)} %get-tuple-element.218), channel_id=1, source_target_pairs={{0,113},{16,97},{32,81},{48,65},{64,49},{80,33},{96,17},{112,1},{1... | collective-permute-start | bytes 491528 | tf_op jit(solution)/shard_map/ppermute | solution.py:319
  436.6 12.1 %collective-permute-start.131 = (bf16[64,1280]{1,0:T(8,128)(2,1)S(1)}, bf16[64,1280]{1,0:T(8,128)(2,1)S(1)}, u32[]{:S(2)}, u32[]{:S(2)}) collective-permute-start(bf16[64,1280]{1,0:T(8,128)(2,1)S(1)} %get-tuple-element.219), channel_id=1, source_target_pairs={{0,112},{16,96},{32,80},{48,64},{64,48},{80,32},{96,16},{112,0},{1... | collective-permute-start | bytes 491528 | tf_op jit(solution)/shard_map/ppermute | solution.py:319
  440.3 11.0 %collective-permute-start.130 = (bf16[64,1280]{1,0:T(8,128)(2,1)S(1)}, bf16[64,1280]{1,0:T(8,128)(2,1)S(1)}, u32[]{:S(2)}, u32[]{:S(2)}) collective-permute-start(bf16[64,1280]{1,0:T(8,128)(2,1)S(1)} %get-tuple-element.216), channel_id=1, source_target_pairs={{0,1},{1,0},{2,3},{3,2},{4,5},{5,4},{6,7},{7,6},{8,9},{9,8},{10,11... | collective-permute-start | bytes 491528 | tf_op jit(solution)/shard_map/ppermute | solution.py:323
  453.1 19.2 %collective-permute-start.136 = (bf16[64,2304]{1,0:T(8,128)(2,1)S(1)}, bf16[64,2304]{1,0:T(8,128)(2,1)S(1)}, u32[]{:S(2)}, u32[]{:S(2)}) collective-permute-start(bf16[64,2304]{1,0:T(8,128)(2,1)S(1)} %get-tuple-element.249), channel_id=1, source_target_pairs={{0,113},{16,97},{32,81},{48,65},{64,49},{80,33},{96,17},{112,1},{1... | collective-permute-start | bytes 884744 | tf_op jit(solution)/shard_map/ppermute | solution.py:319
  453.2 19.1 %collective-permute-start.135 = (bf16[64,2304]{1,0:T(8,128)(2,1)S(1)}, bf16[64,2304]{1,0:T(8,128)(2,1)S(1)}, u32[]{:S(2)}, u32[]{:S(2)}) collective-permute-start(bf16[64,2304]{1,0:T(8,128)(2,1)S(1)} %get-tuple-element.249), channel_id=1, source_target_pairs={{0,112},{16,96},{32,80},{48,64},{64,48},{80,32},{96,16},{112,0},{1... | collective-permute-start | bytes 884744 | tf_op jit(solution)/shard_map/ppermute | solution.py:319
  454.2 20.2 %collective-permute-start.134 = (bf16[64,2304]{1,0:T(8,128)(2,1)S(1)}, bf16[64,2304]{1,0:T(8,128)(2,1)S(1)}, u32[]{:S(2)}, u32[]{:S(2)}) collective-permute-start(bf16[64,2304]{1,0:T(8,128)(2,1)S(1)} %get-tuple-element.250.refs_10_), channel_id=1, source_target_pairs={{0,1},{1,0},{2,3},{3,2},{4,5},{5,4},{6,7},{7,6},{8,9},{9,8},{10,11... | collective-permute-start | bytes 884744 | tf_op jit(solution)/shard_map/ppermute | solution.py:323
  (120 other events, 660.6 us)
